TPU v7x, 32 devices: a whole 2x2x4 slice. The times are simulated.
32 devices in a mesh: orient: 8 (over y, x, core), strip: 4 (over z).
Axes of the slice: x: 2, y: 2, z: 4, core: 2. Of those that a mesh axis runs over, the one named last changes fastest.
Arguments:
- inflow_field: bfloat16 [32, 8, 32, 512], P('orient', None, 'strip'), may hold values from -6 to 6
- kernel_one: bfloat16 [32, 9, 8, 8], replicated, may hold values from -0.125 to 0.125
- kernel_two: bfloat16 [32, 9, 8, 8], replicated, may hold values from -0.125 to 0.125
- turbine_mask: int32 [32, 512], P('strip'), may hold values 0 or 1
- wind_sector: int32 [1], replicated, may hold values from 0 to 31
- wake_cotangent: bfloat16 [32, 8, 32, 512], P('orient', None, 'strip'), may hold values from -6 to 6
Outputs:
- wake_out: bfloat16 [32, 8, 32, 512], P('orient', None, 'strip')
- kernel_grad_one: float32 [32, 9, 8, 8], replicated
- kernel_grad_two: float32 [32, 9, 8, 8], replicated
Inputs may be any that keep to these rules, and one draw needn't show every extreme that they name: `wind_sector`: names one element of the group.
All inputs are finite; a program needn't handle non-finite values. No bound on the sum of `turbine_mask` on one device may be relied on, other than what follows from the above.
Results may differ from a plain program's by a relative error of at most 0.0051.
Values may be sent and summed in bfloat16 or wider, within the bound.
A program may use at most 128 MiB of HBM per device.

v0:
```python
import math

import jax
import jax.numpy as jnp
from jax import lax
from jax.sharding import PartitionSpec as P

G = 32


OFFSETS = ((0, 0), (0, 1), (0, 2), (1, 0), (1, 1), (1, 2), (2, 0), (2, 1), (2, 2))


def with_halo(shard, sides, width):
    for axis, dim in sides:
        count, length = (lax.axis_size(axis), shard.shape[dim])
        up = [(i, (i + 1) % count) for i in range(count - 1)]
        down = [(j, i) for i, j in up]
        last = lax.slice_in_dim(shard, length - width, length, axis=dim)
        first = lax.slice_in_dim(shard, 0, width, axis=dim)
        before = lax.ppermute(last, axis, up)
        after = lax.ppermute(first, axis, down)
        shard = jnp.concatenate([before, shard, after], axis=dim)
    return shard


def relative(row_ids, col_ids, sector):
    halfway = G // 2
    row_rot = row_ids % halfway
    row_ref = row_ids // halfway
    col_rot = col_ids % halfway
    col_ref = col_ids // halfway
    sec_rot = sector % halfway
    sec_ref = sector // halfway
    moved_rot = (sec_rot + (1 - 2 * sec_ref) * col_rot) % halfway
    moved_ref = (sec_ref + col_ref) % 2
    inverse_rot = jnp.where(row_ref == 0, (halfway - row_rot) % halfway, row_rot)
    result_rot = (inverse_rot + (1 - 2 * row_ref) * moved_rot) % halfway
    result_ref = (row_ref + moved_ref) % 2
    return result_ref * halfway + result_rot


def kernel_block(kernel, row_ids, col_ids, sector):
    channels = kernel.shape[2]
    tap_count = kernel.shape[1]
    relation = relative(row_ids[:, None], col_ids[None, :], sector).reshape(-1)
    onehot = (relation[:, None] == jnp.arange(G, dtype=jnp.int32)[None, :]).astype(jnp.bfloat16)
    picked = jnp.dot(onehot, kernel.reshape(G, -1), preferred_element_type=jnp.float32)
    picked = picked.reshape(row_ids.shape[0], col_ids.shape[0], tap_count, channels, channels)
    picked = picked.transpose(2, 0, 3, 1, 4)
    return picked.reshape(
        tap_count, row_ids.shape[0] * channels, col_ids.shape[0] * channels
    ).astype(jnp.bfloat16)


def fold_kernel(partial_grad, row_ids, col_ids, sector):
    tap_count = partial_grad.shape[0]
    channels = partial_grad.shape[1] // row_ids.shape[0]
    relation = relative(row_ids[:, None], col_ids[None, :], sector).reshape(-1)
    onehot = (relation[:, None] == jnp.arange(G, dtype=jnp.int32)[None, :]).astype(jnp.float32)
    arranged = partial_grad.reshape(
        tap_count, row_ids.shape[0], channels, col_ids.shape[0], channels
    )
    arranged = arranged.transpose(1, 3, 0, 2, 4).reshape(relation.shape[0], -1)
    folded = jnp.dot(
        onehot.T, arranged, precision=lax.Precision.HIGHEST, preferred_element_type=jnp.float32
    )
    return folded.reshape(G, tap_count, channels, channels)


def place_forward(mixed_taps, height, extent):
    padded = jnp.pad(mixed_taps, ((0, 0), (0, 0), (0, 0), (1, 1)))
    summed = jnp.zeros((mixed_taps.shape[1], height, extent), jnp.float32)
    for tap_index, (row_shift, col_shift) in enumerate(OFFSETS):
        summed = (
            summed
            + padded[tap_index, :, row_shift : row_shift + height, col_shift : col_shift + extent]
        )
    return summed


def place_backward(mixed_taps, height, extent):
    padded = jnp.pad(mixed_taps, ((0, 0), (0, 0), (0, 0), (1, 1)))
    summed = jnp.zeros((mixed_taps.shape[1], height, extent), jnp.float32)
    for tap_index, (row_shift, col_shift) in enumerate(OFFSETS):
        summed = (
            summed
            + padded[
                tap_index,
                :,
                2 - row_shift : 2 - row_shift + height,
                2 - col_shift : 2 - col_shift + extent,
            ]
        )
    return summed


def layer_forward(source, weights_row):
    tap_count, local_width, full_width = weights_row.shape
    height, extent = (source.shape[1], source.shape[2])
    matrix = weights_row.reshape(tap_count * local_width, full_width)
    widened = with_halo(source, (("strip", 1),), 1)
    gathered = lax.all_gather(widened, "orient", axis=0, tiled=True)
    mixed_taps = jnp.dot(
        matrix, gathered.reshape(full_width, -1), preferred_element_type=jnp.float32
    )
    mixed_taps = mixed_taps.reshape(tap_count, local_width, gathered.shape[1], extent)
    center = gathered[:, 1 : height + 1]
    return (place_forward(mixed_taps, height, extent), center)


def rim_rows(gradient):
    return with_halo(gradient, (("strip", 1),), 1)


def weight_grad(cot_rows, center):
    height, extent = (center.shape[1], center.shape[2])
    padded = jnp.pad(cot_rows, ((0, 0), (0, 0), (1, 1)))
    flat_center = center.reshape(center.shape[0], -1)
    pieces = []
    for row_shift, col_shift in OFFSETS:
        window = padded[
            :, 2 - row_shift : 2 - row_shift + height, 2 - col_shift : 2 - col_shift + extent
        ]
        window = window.reshape(cot_rows.shape[0], -1)
        pieces.append(
            lax.dot_general(
                window, flat_center, (((1,), (1,)), ((), ())), preferred_element_type=jnp.float32
            )
        )
    return jnp.stack(pieces, 0)


def shards(inflow_field, kernel_one, kernel_two, turbine_mask, wind_sector, wake_cotangent):
    groups, channels, height, extent = inflow_field.shape
    local_width = groups * channels
    sector = wind_sector[0]
    neutral = jnp.int32(0)
    all_groups = jnp.arange(G, dtype=jnp.int32)
    scale_factor = 1.0 / math.sqrt(G * height * lax.axis_size("strip") * extent)
    first_group = lax.axis_index("orient") * groups
    my_groups = first_group + jnp.arange(groups, dtype=jnp.int32)
    row_one = kernel_block(kernel_one, my_groups, all_groups, sector)
    row_two = kernel_block(kernel_two, my_groups, all_groups, neutral)
    open_cells = (1 - turbine_mask).astype(jnp.float32)
    source = inflow_field.reshape(local_width, height, extent)
    first_pre, first_center = layer_forward(source, row_one)
    sigmoid_one = jax.nn.sigmoid(first_pre)
    hidden = (first_pre * sigmoid_one * open_cells).astype(jnp.bfloat16)
    second_pre, second_center = layer_forward(hidden, row_two)
    wake_out = second_pre.astype(jnp.bfloat16).reshape(groups, channels, height, extent)
    cotangent = wake_cotangent.reshape(local_width, height, extent)
    cot_two = rim_rows(cotangent)
    grad_two = weight_grad(cot_two, second_center)
    rows_turned = row_two.transpose(0, 2, 1)
    mixed_taps = jnp.dot(
        rows_turned.reshape(9 * (local_width * lax.axis_size("orient")), local_width),
        cot_two.reshape(local_width, -1),
        preferred_element_type=jnp.float32,
    )
    mixed_taps = mixed_taps.reshape(9, local_width * lax.axis_size("orient"), height + 2, extent)
    back_grad = lax.psum_scatter(
        place_backward(mixed_taps, height, extent), "orient", scatter_dimension=0, tiled=True
    )
    first_grad = (
        back_grad * open_cells * sigmoid_one * (1.0 + first_pre * (1.0 - sigmoid_one))
    ).astype(jnp.bfloat16)
    cot_one = rim_rows(first_grad)
    grad_one = weight_grad(cot_one, first_center)
    share_one = fold_kernel(grad_one, my_groups, all_groups, sector) * scale_factor
    share_two = fold_kernel(grad_two, my_groups, all_groups, neutral) * scale_factor
    summed_one, summed_two = lax.psum((share_one, share_two), ("orient", "strip"))
    return (wake_out, summed_one, summed_two)


def solution(mesh):
    return jax.shard_map(
        shards,
        mesh=mesh,
        in_specs=(
            P("orient", None, "strip", None),
            P(),
            P(),
            P("strip", None),
            P(),
            P("orient", None, "strip", None),
        ),
        out_specs=(P("orient", None, "strip", None), P(), P()),
        check_vma=False,
    )
```

profile of v0, /device:TPU:0, one launch (start us, length us, event | category | flops | bytes accessed | tf_op | source)
XLA Modules:
  0.0 375.3 jit_solution(17403840990609357663)
XLA Ops:
  7.2 1.1 copy.98
  8.3 4.9 %collective-permute-start = (bf16[32,1,512]{2,0,1:T(8,128)(2,1)S(1)}, bf16[32,1,512]{2,0,1:T(8,128)(2,1)S(1)}, u32[]{:S(2)}, u32[]{:S(2)}) collective-permute-start(bf16[32,1,512]{2,0,1:T(8,128)(2,1)S(1)} %get-tuple-element.22), channel_id=1, source_target_pairs={{0,1},{1,2},{2,3},{4,5},{5,6},{6,7},{8,9},{9,10},{10,11},{12,13},{... | collective-permute-start | bytes 98312 | tf_op jit(solution)/shard_map/ppermute | solution.py:21
  13.2 1.3 collective-permute-start.1
  14.8 4.2 %collective-permute-done.1 = bf16[32,1,512]{2,0,1:T(8,128)(2,1)S(1)} collective-permute-done((bf16[32,1,512]{2,0,1:T(8,128)(2,1)S(1)}, bf16[32,1,512]{2,0,1:T(8,128)(2,1)S(1)}, u32[]{:S(2)}, u32[]{:S(2)}) %collective-permute-start.1) | collective-permute-done | bytes 32800 | tf_op jit(solution)/shard_map/ppermute | solution.py:22
  21.6 3.5 collective-permute-start.4
  25.1 1.3 collective-permute-start.5
  28.4 1.9 copy.32
  30.3 3.5 convert_element_type.51
  34.7 18.8 %fusion.56 = f32[9,256,10,512]{3,1,2,0:T(8,128)} fusion(bf16[9,32,256]{2,1,0:T(8,128)(2,1)S(1)} %convert_element_type.51, bf16[10,4,8,512]{3,2,1,0:T(8,128)(2,1)S(1)} %get-tuple-element.17), kind=kOutput, calls=%fused_computation.108 | convolution fusion | flops 754974720 | bytes 47661056 | tf_op jit(solution)/shard_map/dot_general | solution.py:156
  53.5 17.2 %fusion.8 = f32[256,8,512]{2,0,1:T(8,128)} fusion(f32[9,256,10,512]{3,1,2,0:T(8,128)} %fusion.56), kind=kLoop, calls=%fused_computation.26 | loop fusion | flops 8388608 | bytes 63963136 | tf_op jit(solution)/shard_map/add | solution.py:87
  71.6 1.2 fusion.14
  72.8 2.8 copy.34
  75.6 4.3 %reshape.552 = bf16[9,32,256,1]{2,1,0,3:T(8,128)(2,1)S(1)} reshape(bf16[9,4,8,32,8]{4,3,2,1,0:T(8,128)(2,1)} %copy.34) | data formatting | bytes 294912 | tf_op jit(solution)/shard_map/convert_element_type | solution.py:53
  79.9 4.7 %copy.36 = bf16[256,10,512]{0,2,1:T(8,128)(2,1)} copy(bf16[256,10,512]{2,0,1:T(8,128)(2,1)} %all-gather.3.cloned.1.call-done) | data formatting | bytes 5242880 | tf_op jit(solution)/shard_map/all_gather | solution.py:103
  84.6 5.3 %fusion.11 = f32[9,32,10,512]{3,1,2,0:T(8,128)} fusion(bf16[256,10,512]{0,2,1:T(8,128)(2,1)} %copy.36, bf16[9,32,256,1]{2,1,0,3:T(8,128)(2,1)S(1)} %reshape.552), kind=kOutput, calls=%fused_computation.29 | convolution fusion | flops 754974720 | bytes 8667136 | tf_op jit(solution)/shard_map/dot_general | solution.py:104
  89.9 33.5 %reduce-scatter.2.cloned.1.call-done = f32[32,8,512]{2,0,1:T(8,128)} async-done(((f32[256,8,512]{2,0,1:T(8,128)}), f32[32,8,512]{2,0,1:T(8,128)}) %reduce-scatter.2.cloned.1.call-update) | async-done | bytes 524304 | tf_op jit(solution)/shard_map/reduce_scatter | solution.py:162
  123.4 3.4 fusion.39
  127.0 3.4 collective-permute-start.2
  130.4 1.3 collective-permute-start.3
  132.0 4.2 %collective-permute-done.3 = bf16[32,1,512]{2,0,1:T(8,128)(2,1)S(1)} collective-permute-done((bf16[32,1,512]{2,0,1:T(8,128)(2,1)S(1)}, bf16[32,1,512]{2,0,1:T(8,128)(2,1)S(1)}, u32[]{:S(2)}, u32[]{:S(2)}) %collective-permute-start.3) | collective-permute-done | bytes 32800 | tf_op jit(solution)/shard_map/ppermute | solution.py:22
  137.1 3.5 reshape.554
  142.6 4.0 %collective-permute-start.6 = (bf16[32,1,512]{2,0,1:T(8,128)(2,1)}, bf16[32,1,512]{2,0,1:T(8,128)(2,1)}, u32[]{:S(2)}, u32[]{:S(2)}) collective-permute-start(bf16[32,1,512]{2,0,1:T(8,128)(2,1)} %get-tuple-element.18), channel_id=1, source_target_pairs={{0,1},{1,2},{2,3},{4,5},{5,6},{6,7},{8,9},{9,10},{10,11},{12,13},{... | collective-permute-start | bytes 98312 | tf_op jit(solution)/shard_map/ppermute | solution.py:21
  146.7 1.5 collective-permute-start.7
  148.2 2.9 convolution_bitcast_fusion.14
  151.1 1.1 stack.64
  153.0 2.1 convolution_bitcast_fusion.3
  155.1 1.1 stack.67
  157.0 2.1 convolution_bitcast_fusion.4
  159.1 1.1 stack.61
  164.0 1.7 convolution_bitcast_fusion.16
  166.2 2.3 convolution_bitcast_fusion.15
  168.5 1.1 stack.63
  170.4 2.3 convolution_bitcast_fusion.13
  172.7 1.1 stack.65
  174.6 2.3 convolution_bitcast_fusion.12
  176.9 1.1 stack.66
  178.8 2.3 convolution_bitcast_fusion.11
  181.2 1.1 stack.68
  184.9 1.3 convolution_multiply_fusion.1
  186.2 3.1 convolution_bitcast_fusion.10
  189.3 1.1 stack.70
  191.2 1.6 constant_dynamic-update-slice_fusion.17
  192.8 2.1 convolution_bitcast_fusion.2
  194.9 1.1 stack.71
  196.8 2.3 convolution_bitcast_fusion.9
  199.1 1.1 stack.72
  201.0 2.3 convolution_bitcast_fusion.8
  203.3 1.1 stack.73
  205.3 2.3 convolution_bitcast_fusion
  207.5 1.1 stack.74
  209.4 2.3 convolution_bitcast_fusion.7
  211.7 1.1 stack.75
  213.7 2.5 convolution_bitcast_fusion.6
  216.2 1.1 stack.76
  218.1 2.1 convolution_bitcast_fusion.1
  220.2 1.1 stack.77
  222.2 2.4 convolution_bitcast_fusion.5
  224.5 1.1 stack.78
  231.1 2.0 copy.61
  233.7 1.3 convolution_multiply_fusion
  235.0 3.0 copy.37
  240.7 124.3 %all-reduce.8.cloned.1.call-done = (f32[32,9,8,8]{0,1,3,2:T(8,128)}, f32[32,9,8,8]{0,1,3,2:T(8,128)}) async-done(((f32[32,9,8,8]{0,1,3,2:T(8,128)}, f32[32,9,8,8]{0,1,3,2:T(8,128)}), (f32[32,9,8,8]{0,1,3,2:T(8,128)}, f32[32,9,8,8]{0,1,3,2:T(8,128)})) %all-reduce.8.cloned.1.call-update) | async-done | bytes 147472 | tf_op jit(solution)/shard_map/psum | solution.py:172
  365.0 1.9 copy.64
  366.9 1.9 copy.65
  (143 shorter events, 35.8 us)
Async XLA Ops:
  7.2 20.7 %copy-start.17 = (bf16[32,9,8,8]{0,3,2,1:T(8,128)(2,1)S(1)}, bf16[32,9,8,8]{0,3,2,1:T(8,128)(2,1)}, u32[]{:S(2)}) copy-start(bf16[32,9,8,8]{0,3,2,1:T(8,128)(2,1)} %param.8) | copy-start | bytes 110596
  7.2 72.7 %all-gather.3.cloned.1.call-start = ((), (), s32[]{:S(2)}) async-start(), calls=%async_computation.1 | async-start | bytes 2949120 | tf_op jit(solution)/shard_map/all_gather | solution.py:103
  8.3 6.5 %collective-permute-start = (bf16[32,1,512]{2,0,1:T(8,128)(2,1)S(1)}, bf16[32,1,512]{2,0,1:T(8,128)(2,1)S(1)}, u32[]{:S(2)}, u32[]{:S(2)}) collective-permute-start(bf16[32,1,512]{2,0,1:T(8,128)(2,1)S(1)} %get-tuple-element.22), channel_id=1, source_target_pairs={{0,1},{1,2},{2,3},{4,5},{5,6},{6,7},{8,9},{9,10},{10,11},{12,13},{... | collective-permute-start | bytes 98312 | tf_op jit(solution)/shard_map/ppermute | solution.py:21
  13.2 5.8 %collective-permute-start.1 = (bf16[32,1,512]{2,0,1:T(8,128)(2,1)S(1)}, bf16[32,1,512]{2,0,1:T(8,128)(2,1)S(1)}, u32[]{:S(2)}, u32[]{:S(2)}) collective-permute-start(bf16[32,1,512]{2,0,1:T(8,128)(2,1)S(1)} %get-tuple-element.23), channel_id=1, source_target_pairs={{1,0},{2,1},{3,2},{5,4},{6,5},{7,6},{9,8},{10,9},{11,10},{13,12},{... | collective-permute-start | bytes 98312 | tf_op jit(solution)/shard_map/ppermute | solution.py:22
  19.9 103.6 %reduce-scatter.2.cloned.1.call-start = ((), (), s32[]{:S(2)}) async-start(), calls=%async_computation.3 | async-start | bytes 4718592 | tf_op jit(solution)/shard_map/reduce_scatter | solution.py:162
  20.9 0.7 copy-start.2
  21.6 12.2 %collective-permute-start.4 = (bf16[32,1,512]{2,0,1:T(8,128)(2,1)S(1)}, bf16[32,1,512]{2,0,1:T(8,128)(2,1)S(1)}, u32[]{:S(2)}, u32[]{:S(2)}) collective-permute-start(bf16[32,1,512]{2,0,1:T(8,128)(2,1)S(1)} %get-tuple-element.24), channel_id=1, source_target_pairs={{0,1},{1,2},{2,3},{4,5},{5,6},{6,7},{8,9},{9,10},{10,11},{12,13},{... | collective-permute-start | bytes 98312 | tf_op jit(solution)/shard_map/ppermute | solution.py:21
  25.1 8.7 %collective-permute-start.5 = (bf16[32,1,512]{2,0,1:T(8,128)(2,1)S(1)}, bf16[32,1,512]{2,0,1:T(8,128)(2,1)S(1)}, u32[]{:S(2)}, u32[]{:S(2)}) collective-permute-start(bf16[32,1,512]{2,0,1:T(8,128)(2,1)S(1)} %get-tuple-element.25), channel_id=1, source_target_pairs={{1,0},{2,1},{3,2},{5,4},{6,5},{7,6},{9,8},{10,9},{11,10},{13,12},{... | collective-permute-start | bytes 98312 | tf_op jit(solution)/shard_map/ppermute | solution.py:22
  30.3 3.6 copy-start.3
  33.9 19.6 %copy-start.21 = (bf16[32,1,512]{2,0,1:T(8,128)(2,1)}, bf16[32,1,512]{2,0,1:T(8,128)(2,1)S(1)}, u32[]{:S(2)}) copy-start(bf16[32,1,512]{2,0,1:T(8,128)(2,1)S(1)} %collective-permute-done.4) | copy-start | bytes 98308
  33.9 19.6 %copy-start.22 = (bf16[32,1,512]{2,0,1:T(8,128)(2,1)}, bf16[32,1,512]{2,0,1:T(8,128)(2,1)S(1)}, u32[]{:S(2)}) copy-start(bf16[32,1,512]{2,0,1:T(8,128)(2,1)S(1)} %collective-permute-done.5) | copy-start | bytes 98308
  70.7 0.9 copy-start.18
  70.7 115.6 %all-gather.5.cloned.1.call-start = ((), (), s32[]{:S(2)}) async-start(), calls=%async_computation.2 | async-start | bytes 2949120 | tf_op jit(solution)/shard_map/all_gather | solution.py:103
  75.6 4.3 %copy-start.23 = (s32[8,512]{1,0:T(8,128)S(1)}, s32[8,512]{1,0:T(8,128)}, u32[]{:S(2)}) copy-start(s32[8,512]{1,0:T(8,128)} %param.9) | copy-start | bytes 49156
  126.8 13.8 %copy-start.27 = (s32[4,32]{1,0:T(4,128)S(1)}, s32[4,32]{1,0:T(4,128)}, u32[]{:S(2)}) copy-start(s32[4,32]{1,0:T(4,128)} %get-tuple-element.31) | copy-start | bytes 1540
  126.8 13.9 %copy-start.26 = (s32[4,32]{1,0:T(4,128)S(1)}, s32[4,32]{1,0:T(4,128)}, u32[]{:S(2)}) copy-start(s32[4,32]{1,0:T(4,128)} %get-tuple-element.26) | copy-start | bytes 1540
  126.8 14.0 %copy-start.25 = (s32[4,32]{1,0:T(4,128)S(1)}, s32[4,32]{1,0:T(4,128)}, u32[]{:S(2)}) copy-start(s32[4,32]{1,0:T(4,128)} %get-tuple-element.30) | copy-start | bytes 1540
  126.8 14.0 %copy-start.24 = (s32[4,32]{1,0:T(4,128)S(1)}, s32[4,32]{1,0:T(4,128)}, u32[]{:S(2)}) copy-start(s32[4,32]{1,0:T(4,128)} %get-tuple-element.29) | copy-start | bytes 1540
  127.0 5.0 %collective-permute-start.2 = (bf16[32,1,512]{2,0,1:T(8,128)(2,1)S(1)}, bf16[32,1,512]{2,0,1:T(8,128)(2,1)S(1)}, u32[]{:S(2)}, u32[]{:S(2)}) collective-permute-start(bf16[32,1,512]{2,0,1:T(8,128)(2,1)S(1)} %get-tuple-element.20), channel_id=1, source_target_pairs={{0,1},{1,2},{2,3},{4,5},{5,6},{6,7},{8,9},{9,10},{10,11},{12,13},{... | collective-permute-start | bytes 98312 | tf_op jit(solution)/shard_map/ppermute | solution.py:21
  130.4 5.8 %collective-permute-start.3 = (bf16[32,1,512]{2,0,1:T(8,128)(2,1)S(1)}, bf16[32,1,512]{2,0,1:T(8,128)(2,1)S(1)}, u32[]{:S(2)}, u32[]{:S(2)}) collective-permute-start(bf16[32,1,512]{2,0,1:T(8,128)(2,1)S(1)} %get-tuple-element.21), channel_id=1, source_target_pairs={{1,0},{2,1},{3,2},{5,4},{6,5},{7,6},{9,8},{10,9},{11,10},{13,12},{... | collective-permute-start | bytes 98312 | tf_op jit(solution)/shard_map/ppermute | solution.py:22
  137.0 228.0 %all-reduce.8.cloned.1.call-start = ((), (), s32[]{:S(2)}) async-start(), calls=%async_computation.4 | async-start | bytes 2097152 | tf_op jit(solution)/shard_map/psum | solution.py:172
  140.6 12.4 %copy-start.1 = (bf16[256,10,512]{2,0,1:T(8,128)(2,1)S(1)}, bf16[256,10,512]{2,0,1:T(8,128)(2,1)}, u32[]{:S(2)}) copy-start(bf16[256,10,512]{2,0,1:T(8,128)(2,1)} %all-gather.3.cloned.1.call-done) | copy-start | bytes 7864324
  142.6 10.3 %collective-permute-start.6 = (bf16[32,1,512]{2,0,1:T(8,128)(2,1)}, bf16[32,1,512]{2,0,1:T(8,128)(2,1)}, u32[]{:S(2)}, u32[]{:S(2)}) collective-permute-start(bf16[32,1,512]{2,0,1:T(8,128)(2,1)} %get-tuple-element.18), channel_id=1, source_target_pairs={{0,1},{1,2},{2,3},{4,5},{5,6},{6,7},{8,9},{9,10},{10,11},{12,13},{... | collective-permute-start | bytes 98312 | tf_op jit(solution)/shard_map/ppermute | solution.py:21
  146.7 10.4 %collective-permute-start.7 = (bf16[32,1,512]{2,0,1:T(8,128)(2,1)}, bf16[32,1,512]{2,0,1:T(8,128)(2,1)}, u32[]{:S(2)}, u32[]{:S(2)}) collective-permute-start(bf16[32,1,512]{2,0,1:T(8,128)(2,1)} %get-tuple-element.19), channel_id=1, source_target_pairs={{1,0},{2,1},{3,2},{5,4},{6,5},{7,6},{9,8},{10,9},{11,10},{13,12},{... | collective-permute-start | bytes 98312 | tf_op jit(solution)/shard_map/ppermute | solution.py:22
  162.0 0.7 copy-start.19
  178.8 3.7 copy-start.8
  178.8 4.6 %copy-start.5 = (f32[1,4,8,32,8]{3,4,2,1,0:T(8,128)S(1)}, f32[1,4,8,32,8]{3,4,2,1,0:T(8,128)}, u32[]{:S(2)}) copy-start(f32[1,4,8,32,8]{3,4,2,1,0:T(8,128)} %copy.45) | copy-start | bytes 98308
  178.8 4.7 %copy-start.14 = (f32[1,4,8,32,8]{3,4,2,1,0:T(8,128)S(1)}, f32[1,4,8,32,8]{3,4,2,1,0:T(8,128)}, u32[]{:S(2)}) copy-start(f32[1,4,8,32,8]{3,4,2,1,0:T(8,128)} %copy.46) | copy-start | bytes 98308
  181.2 2.4 copy-start.15
  181.2 2.4 copy-start.6
  183.6 1.3 copy-start.29
  183.6 2.6 copy-start.20
  186.2 6.6 %copy-start.4 = (bf16[4,8,8,512]{3,1,0,2:T(8,128)(2,1)S(1)}, bf16[4,8,8,512]{3,1,0,2:T(8,128)(2,1)}, u32[]{:S(2)}) copy-start(bf16[4,8,8,512]{3,1,0,2:T(8,128)(2,1)} %copy-done.2) | copy-start | bytes 786436
  186.2 6.6 %copy-start = (bf16[256,10,512]{2,0,1:T(8,128)(2,1)S(1)}, bf16[256,10,512]{2,0,1:T(8,128)(2,1)}, u32[]{:S(2)}) copy-start(bf16[256,10,512]{2,0,1:T(8,128)(2,1)} %all-gather.5.cloned.1.call-done) | copy-start | bytes 7864324
  221.3 4.5 %copy-start.7 = (f32[1,4,8,32,8]{3,4,2,1,0:T(8,128)S(1)}, f32[1,4,8,32,8]{3,4,2,1,0:T(8,128)}, u32[]{:S(2)}) copy-start(f32[1,4,8,32,8]{3,4,2,1,0:T(8,128)} %copy.53) | copy-start | bytes 98308
  222.1 4.4 %copy-start.9 = (f32[1,4,8,32,8]{3,4,2,1,0:T(8,128)S(1)}, f32[1,4,8,32,8]{3,4,2,1,0:T(8,128)}, u32[]{:S(2)}) copy-start(f32[1,4,8,32,8]{3,4,2,1,0:T(8,128)} %copy.54) | copy-start | bytes 98308
  222.1 5.0 %copy-start.10 = (f32[1,4,8,32,8]{3,4,2,1,0:T(8,128)S(1)}, f32[1,4,8,32,8]{3,4,2,1,0:T(8,128)}, u32[]{:S(2)}) copy-start(f32[1,4,8,32,8]{3,4,2,1,0:T(8,128)} %copy.55) | copy-start | bytes 98308
  222.1 5.7 %copy-start.11 = (f32[1,4,8,32,8]{3,4,2,1,0:T(8,128)S(1)}, f32[1,4,8,32,8]{3,4,2,1,0:T(8,128)}, u32[]{:S(2)}) copy-start(f32[1,4,8,32,8]{3,4,2,1,0:T(8,128)} %copy.56) | copy-start | bytes 98308
  222.2 6.3 %copy-start.12 = (f32[1,4,8,32,8]{3,4,2,1,0:T(8,128)S(1)}, f32[1,4,8,32,8]{3,4,2,1,0:T(8,128)}, u32[]{:S(2)}) copy-start(f32[1,4,8,32,8]{3,4,2,1,0:T(8,128)} %copy.57) | copy-start | bytes 98308
  222.2 7.0 %copy-start.13 = (f32[1,4,8,32,8]{3,4,2,1,0:T(8,128)S(1)}, f32[1,4,8,32,8]{3,4,2,1,0:T(8,128)}, u32[]{:S(2)}) copy-start(f32[1,4,8,32,8]{3,4,2,1,0:T(8,128)} %copy.58) | copy-start | bytes 98308
  224.5 5.3 %copy-start.16 = (f32[1,4,8,32,8]{3,4,2,1,0:T(8,128)S(1)}, f32[1,4,8,32,8]{3,4,2,1,0:T(8,128)}, u32[]{:S(2)}) copy-start(f32[1,4,8,32,8]{3,4,2,1,0:T(8,128)} %copy.59) | copy-start | bytes 98308
  230.5 3.2 copy-start.28
Sparse Core Ops, SparseCore 0:
  20.0 30.3 all-gather.2
  70.8 52.5 reduce-scatter.1
  137.1 29.1 all-gather.4
  235.2 129.8 all-reduce.7
where the time goes:
time: 378 us; the launch traced here: 375 us
  waiting for transfers between devices  167 us (44%)
  local copies, waits for them, and re-layouts  75.7 us (20%)
  matrix products  69.3 us (18%)
  other arithmetic  26.7 us (7%)
  starting transfers between devices  21.5 us (6%)
  between operations  15.1 us (4%)
    psum x1, waiting for transfers between devices, shards(): lax.psum((share_one, share_two), ('orient', 'strip'))  124 us
    dot_general x18, matrix products, weight_grad(): lax.dot_general(window, flat_center, (((1,), (1,)), ((), ())), preferred_...  39.9 us
    reduce_scatter x1, waiting for transfers between devices, shards(): lax.psum_scatter(place_backward(mixed_taps, height, extent), 'orient', sc...  33.5 us
    another operation x38, local copies, waits for them, and re-layouts, weight_grad(): return jnp.stack(pieces, 0)  31.1 us
    dot_general x1, matrix products, shards(): jnp.dot(rows_turned.reshape(9 * (local_width * lax.axis_size('orient')),...  18.8 us
    add x1, other arithmetic, place_backward(): summed + padded[tap_index, :, 2 - row_shift:2 - row_shift + height, 2 - c...  17.2 us
    unnamed x81, local copies, waits for them, and re-layouts  16.1 us
    convert_element_type x5, local copies, waits for them, and re-layouts, kernel_block(): return picked.reshape(tap_count, row_ids.shape[0] * channels, col_ids.sha...  16 us
  transfers between devices with their start and end apart: 12, of which 6 were waited for; matrix products, arithmetic and copies ran while one was open for 30% of the time, Pallas kernels for 0%

commit v1 on v0

v1 whole, which is shorter than its diff:
```python
import functools
import math

import jax
import jax.numpy as jnp
from jax import lax
from jax.experimental import pallas as pl
from jax.experimental.pallas import tpu as pltpu
from jax.sharding import PartitionSpec as P

G = 32
HALF = 16
LANES = 128
BF16 = jnp.bfloat16
F32 = jnp.float32


def relative(row_ids, col_ids, sector):
    row_rot = row_ids % HALF
    row_ref = row_ids // HALF
    col_rot = col_ids % HALF
    col_ref = col_ids // HALF
    sec_rot = sector % HALF
    sec_ref = sector // HALF
    moved_rot = (sec_rot + (1 - 2 * sec_ref) * col_rot) % HALF
    moved_ref = (sec_ref + col_ref) % 2
    inverse_rot = jnp.where(row_ref == 0, (HALF - row_rot) % HALF, row_rot)
    result_rot = (inverse_rot + (1 - 2 * row_ref) * moved_rot) % HALF
    result_ref = (row_ref + moved_ref) % 2
    return result_ref * HALF + result_rot


def build_weights(bases, at, dst, flip):
    for s in range(2):
        for m in range(dst.shape[1] // LANES):
            cols = slice(m * LANES, (m + 1) * LANES)
            base = bases[at + s, :, cols]
            turned = [base if r == 0 else pltpu.roll(base, 8 * r, 1) for r in range(HALF)]
            if flip is not None:
                turned = [jnp.where(flip, turned[-r % HALF], turned[r]) for r in range(HALF)]
            for r in range(0, HALF, 2):
                both = jnp.concatenate([turned[r], turned[r + 1]], axis=0).astype(BF16)
                row = (s * HALF + r) * 8
                dst[row : row + 16, cols] = both


def fold(product, out, tap_row, flip):
    for b in range(3):
        for sg in range(2):
            lane = slice(sg * LANES, (sg + 1) * LANES)
            for sh in range(2):
                total = None
                for r in range(HALF):
                    row = b * 256 + (sh * HALF + r) * 8
                    piece = product[row : row + 8, lane]
                    if r > 0:
                        back = pltpu.roll(piece, LANES - 8 * r, 1)
                        if flip is not None:
                            back = jnp.where(flip, pltpu.roll(piece, 8 * r, 1), back)
                        piece = back
                    total = piece if total is None else total + piece
                at = (tap_row * 3 + b) * 256 + sg * LANES
                out[sh, :, at : at + LANES] = total


def shifted(value, by):
    if by == 0:
        return value
    return pltpu.roll(value.astype(F32), by % LANES, 1).astype(BF16)


def stack_shifts(src, dst, first, count, sign):
    for i in range(first, first + count):
        cols = slice(i * LANES, (i + 1) * LANES)
        value = src[:, cols]
        for b in range(3):
            dst[b * 256 : (b + 1) * 256, cols] = shifted(value, sign * (1 - b))


def dot(a, b):
    return jnp.dot(a, b, preferred_element_type=F32)


def dot_nt(a, b):
    return lax.dot_general(a, b, (((1,), (1,)), ((), ())), preferred_element_type=F32)


def compute(width, bases, turn, opened, x, cot, wake, t1, t2, w1, w2, w2t, xs, hs, cs, dfac, hid, own, prod):
    flip = turn[...] > 0.5
    build_weights(bases, 0, w1, flip)
    build_weights(bases, 2, w2, None)
    build_weights(bases, 4, w2t, None)
    lane = lax.broadcasted_iota(jnp.int32, (256, LANES), 1)
    inner = (lane >= 2) & (lane < 2 + width)
    stack_shifts(x, xs, 0, 12, 1)
    for n in range(5):
        total = sum(
            dot(w1[:, a * 768 : (a + 1) * 768], xs[:, (2 * n + a) * LANES : (2 * n + a + 2) * LANES])
            for a in range(3)
        )
        cols = slice(2 * n * LANES, (2 * n + 2) * LANES)
        free = opened[0:1, cols]
        sig = jax.nn.sigmoid(total)
        hid[:, cols] = (total * sig * free).astype(BF16)
        dfac[:, cols] = free * sig * (1.0 + total * (1.0 - sig))
    stack_shifts(hid, hs, 0, 10, 1)
    for n in range(4):
        total = sum(
            dot(w2[:, a * 768 : (a + 1) * 768], hs[:, (2 * n + a) * LANES : (2 * n + a + 2) * LANES])
            for a in range(3)
        )
        wake[:, 2 * n * LANES : (2 * n + 2) * LANES] = total.astype(BF16)
    stack_shifts(cot, cs, 0, 10, -1)
    for i in range(8):
        value = cot[:, (i + 1) * LANES : (i + 2) * LANES].astype(F32)
        own[:, i * LANES : (i + 1) * LANES] = jnp.where(inner, value, 0.0).astype(BF16)
    for a in range(3):
        prod[...] = dot_nt(hs[:, a * LANES : (a + 8) * LANES], own[...])
        fold(prod, t2, a, None)
    for n in range(4):
        total = sum(
            dot(
                w2t[:, a * 768 : (a + 1) * 768],
                cs[:, (2 * n + 2 - a) * LANES : (2 * n + 4 - a) * LANES],
            )
            for a in range(3)
        )
        cols = slice((2 * n + 1) * LANES, (2 * n + 3) * LANES)
        total = total * dfac[:, cols]
        for i in range(2):
            value = jnp.where(inner, total[:, i * LANES : (i + 1) * LANES], 0.0)
            own[:, (2 * n + i) * LANES : (2 * n + i + 1) * LANES] = value.astype(BF16)
    for a in range(3):
        prod[...] = dot_nt(xs[:, (a + 1) * LANES : (a + 9) * LANES], own[...])
        fold(prod, t1, a, flip)


def local_kernel(width, bases, turn, opened, x, cot):
    vmem = pl.BlockSpec(memory_space=pltpu.VMEM)
    return pl.pallas_call(
        functools.partial(compute, width),
        out_shape=(
            jax.ShapeDtypeStruct((256, 8 * LANES), BF16),
            jax.ShapeDtypeStruct((2, 8, 2304), F32),
            jax.ShapeDtypeStruct((2, 8, 2304), F32),
        ),
        in_specs=[vmem] * 5,
        out_specs=(vmem,) * 3,
        scratch_shapes=[
            pltpu.VMEM((256, 2304), BF16),
            pltpu.VMEM((256, 2304), BF16),
            pltpu.VMEM((256, 2304), BF16),
            pltpu.VMEM((768, 12 * LANES), BF16),
            pltpu.VMEM((768, 10 * LANES), BF16),
            pltpu.VMEM((768, 10 * LANES), BF16),
            pltpu.VMEM((256, 10 * LANES), F32),
            pltpu.VMEM((256, 10 * LANES), BF16),
            pltpu.VMEM((256, 8 * LANES), BF16),
            pltpu.VMEM((768, 256), F32),
        ],
        compiler_params=pltpu.CompilerParams(vmem_limit_bytes=48 * 1024 * 1024),
    )(bases, turn, opened, x, cot)


def windows(padded, width):
    step = (padded.shape[-1] - 4) // width
    rest = [(0, 0)] * (padded.ndim - 1) + [(0, LANES - step - 4)]
    pieces = [jnp.pad(padded[..., step * i : step * i + step + 4], rest) for i in range(width)]
    return jnp.stack(pieces, 0)


def edges(rows, width):
    count = lax.axis_size("strip")
    height = rows.shape[-2]
    up = [(i, i + 1) for i in range(count - 1)]
    down = [(i + 1, i) for i in range(count - 1)]
    before = lax.ppermute(rows[..., height - width :, :], "strip", up)
    after = lax.ppermute(rows[..., :width, :], "strip", down)
    return jnp.concatenate([before, rows, after], axis=-2)


def turned_bank(bank, sector, transposed):
    ids = jnp.arange(G, dtype=jnp.int32)
    pair = jnp.array([0, HALF], jnp.int32)
    if transposed:
        relation = relative(ids[None, :], pair[:, None], sector)
    else:
        relation = relative(pair[:, None], ids[None, :], sector)
    onehot = (relation.reshape(-1)[:, None] == ids[None, :]).astype(BF16)
    picked = jnp.dot(onehot, bank.reshape(G, -1), preferred_element_type=F32)
    picked = picked.reshape(2, G, 9, 8, 8)
    order = (0, 4, 2, 1, 3) if transposed else (0, 3, 2, 1, 4)
    return picked.transpose(order).reshape(2, 8, 2304)


def unfold(folded, sector):
    ids = jnp.arange(HALF, dtype=jnp.int32)
    sec_rot, sec_ref = sector % HALF, sector // HALF
    sh = jnp.arange(2, dtype=jnp.int32)[:, None, None]
    sg = jnp.arange(2, dtype=jnp.int32)[None, :, None]
    j = ids[None, None, :]
    turn = (sh + sec_ref) % 2
    rot = jnp.where(sg == 0, sec_rot - j + HALF, j - sec_rot + HALF) % HALF
    element = (((turn + sg) % 2) * HALF + rot).reshape(-1)
    onehot = (jnp.arange(G, dtype=jnp.int32)[:, None] == element[None, :]).astype(F32)
    parts = folded.reshape(2, 8, 9, 2, HALF, 8).transpose(0, 3, 4, 2, 5, 1).reshape(64, 576)
    full = jnp.dot(onehot, parts, precision=lax.Precision.HIGHEST, preferred_element_type=F32)
    return full.reshape(G, 9, 8, 8)


def shards(inflow_field, kernel_one, kernel_two, turbine_mask, wind_sector, wake_cotangent):
    groups, channels, height, extent = inflow_field.shape
    local = groups * channels
    devices = lax.axis_size("orient")
    sector = wind_sector[0]
    neutral = jnp.int32(0)
    scale = 1.0 / math.sqrt(G * height * lax.axis_size("strip") * extent)
    bases = jnp.concatenate(
        [
            turned_bank(kernel_one, sector, False),
            turned_bank(kernel_two, neutral, False),
            turned_bank(kernel_two, neutral, True),
        ],
        0,
    )
    turn = jnp.broadcast_to((sector // HALF).astype(F32), (8, LANES))
    both = jnp.stack([inflow_field, wake_cotangent], 0).reshape(2, local, height, extent)
    both = jnp.pad(both, ((0, 0), (0, 0), (0, 0), (2, 2)))
    packed = windows(both, devices)
    spread = lax.all_to_all(packed, "orient", 0, 0, tiled=True)
    x = edges(spread[:, 0], 2).reshape(devices * local, -1)
    cot = edges(spread[:, 1], 1).reshape(devices * local, -1)
    free = edges((1 - turbine_mask).astype(F32), 1)
    free = windows(jnp.pad(free, ((0, 0), (2, 2))), devices)
    free = lax.dynamic_index_in_dim(free, lax.axis_index("orient"), 0, keepdims=False)
    opened = jnp.broadcast_to(free.reshape(1, -1), (8, (height + 2) * LANES))
    wake, t1, t2 = local_kernel(extent // devices, bases, turn, opened, x, cot)
    wake = lax.all_to_all(wake.reshape(devices, local, -1), "orient", 0, 0, tiled=True)
    wake = wake.reshape(devices, local, height, LANES)[..., 2 : 2 + extent // devices]
    wake = wake.transpose(1, 2, 0, 3).reshape(groups, channels, height, extent)
    t1, t2 = lax.psum((t1, t2), ("orient", "strip"))
    return (wake, unfold(t1, sector) * scale, unfold(t2, neutral) * scale)


def solution(mesh):
    return jax.shard_map(
        shards,
        mesh=mesh,
        in_specs=(
            P("orient", None, "strip", None),
            P(),
            P(),
            P("strip", None),
            P(),
            P("orient", None, "strip", None),
        ),
        out_specs=(P("orient", None, "strip", None), P(), P()),
        check_vma=False,
    )
```

time: 378 us -> 240 us (0.63)
  matrix products: 69.3 us -> 6.68 us
  local copies, waits for them, and re-layouts: 75.7 us -> 35.2 us
  waiting for transfers between devices: 167 us -> 130 us
  other arithmetic: 26.7 us -> 16.7 us
  Pallas kernels: 0 us -> 8.36 us
  starting transfers between devices: 21.5 us -> 27.6 us
    dot_general x25 -> x5, matrix products: 69.3 us -> 6.68 us  [the longest x3 4.84 us: turned_bank(): picked = jnp.dot(onehot, bank.reshape(G, -1), preferred_element_type=F32)]
    reduce_scatter x1 -> x0, waiting for transfers between devices: 33.5 us -> none  [shards(): lax.psum_scatter(place_backward(mixed_taps, height, extent), 'orient', sc...]
    another operation x38 -> x2, local copies, waits for them, and re-layouts: 31.1 us -> 0.68 us  [windows(): return jnp.stack(pieces, 0)]
    add x4 -> x6, other arithmetic: 18.9 us -> 2.7 us  [the longest x2 1.42 us: relative(): return result_ref * HALF + result_rot]
    convert_element_type x5 -> x0, local copies, waits for them, and re-layouts: 16 us -> none  [kernel_block(): return picked.reshape(tap_count, row_ids.shape[0] * channels, col_ids.sha...]
    reshape x2 -> x8, local copies, waits for them, and re-layouts: 1.03 us -> 13.8 us  [the longest x4 6.87 us: unfold(): folded.reshape(2, 8, 9, 2, HALF, 8).transpose(0, 3, 4, 2, 5, 1)]
    unnamed x81 -> x30, local copies, waits for them, and re-layouts: 16.1 us -> 6.81 us
    pallas_call x0 -> x1, Pallas kernels: none -> 8.36 us  [local_kernel(): pl.pallas_call(functools.partial(compute, width), out_shape=(jax.ShapeDty...]
  transfers between devices with their start and end apart: 12 -> 9, of which waited for: 6 -> 3; matrix products, arithmetic and copies ran while one was open for 30% -> 17% of each run, Pallas kernels for 0% -> 0%
where the time goes in v1:
time: 240 us
  waiting for transfers between devices  130 us (54%)
  local copies, waits for them, and re-layouts  35.2 us (15%)
  starting transfers between devices  27.6 us (12%)
  other arithmetic  16.7 us (7%)
  between operations  15 us (6%)
  Pallas kernels  8.36 us (3%)
  matrix products  6.68 us (3%)
    psum x1, waiting for transfers between devices, shards(): t1, t2 = lax.psum((t1, t2), ('orient', 'strip'))  129 us
    ppermute x3, starting transfers between devices, edges(): before = lax.ppermute(rows[..., height - width:, :], 'strip', up)  15.4 us
    pallas_call x1, Pallas kernels, local_kernel(): pl.pallas_call(functools.partial(compute, width), out_shape=(jax.ShapeDty...  8.36 us
    reshape x4, local copies, waits for them, and re-layouts, unfold(): folded.reshape(2, 8, 9, 2, HALF, 8).transpose(0, 3, 4, 2, 5, 1)  6.87 us
    unnamed x30, local copies, waits for them, and re-layouts  6.81 us
    reshape x3, local copies, waits for them, and re-layouts, turned_bank(): return picked.transpose(order).reshape(2, 8, 2304)  5.95 us
    transpose x3, local copies, waits for them, and re-layouts, turned_bank(): return picked.transpose(order).reshape(2, 8, 2304)  5.62 us
    dot_general x3, matrix products, turned_bank(): picked = jnp.dot(onehot, bank.reshape(G, -1), preferred_element_type=F32)  4.84 us
  transfers between devices with their start and end apart: 9, of which 3 were waited for; matrix products, arithmetic and copies ran while one was open for 17% of the time, Pallas kernels for 0%

profile of v1, /device:TPU:0, one launch (start us, length us, event | category | flops | bytes accessed | tf_op | source)
XLA Modules:
  0.0 239.6 jit_solution(9336219845008203051)
XLA Ops:
  7.2 0.7 subtract_convert_fusion
  7.9 0.6 fusion.61
  8.5 1.3 collective-permute-start.1
  9.8 6.2 %collective-permute-start = (f32[1,512]{1,0:T(1,128)}, f32[1,512]{1,0:T(1,128)}, u32[]{:S(2)}, u32[]{:S(2)}) collective-permute-start(f32[1,512]{1,0:T(1,128)} %get-tuple-element.39), channel_id=1, source_target_pairs={{0,1},{1,2},{2,3},{4,5},{5,6},{6,7},{8,9},{9,10},{10,11},{12,13},{... | collective-permute-start | bytes 6152 | tf_op jit(solution)/shard_map/ppermute | solution.py:177
  15.9 1.1 pad_maximum_fusion.2
  17.0 2.0 fusion.14
  19.2 0.7 fusion.8
  19.9 0.7 bitcast_dynamic-update-slice_fusion.6
  20.6 0.7 bitcast_dynamic-update-slice_fusion.5
  21.3 0.7 bitcast_dynamic-update-slice_fusion.4
  21.9 0.7 bitcast_dynamic-update-slice_fusion.3
  22.6 0.7 bitcast_dynamic-update-slice_fusion.2
  23.3 0.7 bitcast_dynamic-update-slice_fusion.1
  24.0 0.7 bitcast_dynamic-update-slice_fusion
  24.6 4.2 %all-to-all-start = ((bf16[8,2,32,8,128]{4,3,2,1,0:T(8,128)(2,1)}), bf16[8,2,32,8,128]{4,3,2,1,0:T(8,128)(2,1)S(1)}, u32[]{:S(2)}, u32[]{:S(2)}) async-start(bf16[8,2,32,8,128]{4,3,2,1,0:T(8,128)(2,1)} %bitcast_dynamic-update-slice_fusion), calls=%async_computation | async-start | bytes 2097152 | tf_op jit(solution)/shard_map/all_to_all | solution.py:230
  29.6 0.6 compare_select_fusion.39
  30.2 0.5 multiply_subtract_fusion.1
  30.7 0.6 and_select_fusion.12
  31.3 0.6 iota_compare_fusion.5
  31.9 0.6 iota_add_fusion
  32.4 0.5 and_select_fusion.2
  33.1 1.4 convolution_bitcast_fusion
  34.5 1.9 copy.50
  36.4 2.0 reshape.885
  38.3 0.6 and_select_fusion.5
  38.9 0.6 subtract_add_fusion
  39.5 1.3 fusion.32
  40.8 1.4 convolution_bitcast_fusion.1
  42.2 1.9 copy.48
  44.1 2.0 reshape.884
  46.1 2.1 convolution_bitcast_fusion.2
  48.1 1.9 copy.46
  50.0 2.0 reshape.882
  52.0 0.7 fusion.43
  52.8 0.8 and_select_fusion
  53.6 1.0 pad_maximum_fusion.3.bases
  54.6 0.7 fusion.44
  55.4 0.7 pad_maximum_fusion.4
  56.2 0.7 constant_dynamic-update-slice_fusion.7
  57.4 1.3 collective-permute-start.5
  58.7 4.6 %collective-permute-start.4 = (bf16[8,32,1,128]{3,2,1,0:T(2,128)(2,1)S(1)}, bf16[8,32,1,128]{3,2,1,0:T(2,128)(2,1)S(1)}, u32[]{:S(2)}, u32[]{:S(2)}) collective-permute-start(bf16[8,32,1,128]{3,2,1,0:T(2,128)(2,1)S(1)} %get-tuple-element.22), channel_id=1, source_target_pairs={{0,1},{1,2},{2,3},{4,5},{5,6},{6,7},{8,9},{9,10},{10,11},{12,13},{... | collective-permute-start | bytes 196616 | tf_op jit(solution)/shard_map/ppermute | solution.py:177
  63.5 1.3 collective-permute-start.3
  64.8 4.7 %collective-permute-start.2 = (bf16[8,32,2,128]{3,2,1,0:T(2,128)(2,1)S(1)}, bf16[8,32,2,128]{3,2,1,0:T(2,128)(2,1)S(1)}, u32[]{:S(2)}, u32[]{:S(2)}) collective-permute-start(bf16[8,32,2,128]{3,2,1,0:T(2,128)(2,1)S(1)} %get-tuple-element.24), channel_id=1, source_target_pairs={{0,1},{1,2},{2,3},{4,5},{5,6},{6,7},{8,9},{9,10},{10,11},{12,13},{... | collective-permute-start | bytes 393224 | tf_op jit(solution)/shard_map/ppermute | solution.py:177
  69.5 0.7 pad_maximum_fusion.1
  70.4 0.3 collective-permute-done.3
  70.7 1.2 collective-permute-done.2
  71.9 0.6 pad_maximum_fusion
  72.7 8.4 %shard_map.112 = (bf16[256,1024]{1,0:T(8,128)(2,1)}, f32[2,8,2304]{2,1,0:T(8,128)S(1)}, f32[2,8,2304]{2,1,0:T(8,128)S(1)}) custom-call(f32[6,8,2304]{2,1,0:T(8,128)S(1)} %pad_maximum_fusion.3.bases, f32[8,128]{1,0:T(8,128)S(1)} %broadcast_in_dim.66.turn, f32[8,1280]{1,0:T(8,128)S(1)} %broadcast_in_dim.68.opened, bf16[256,1536]{1,0:T(8,128)(2,1)S(1)} %bitcast.145, ...), custom_call_target="tpu_custom_call" | custom-call | tf_op jit(solution)/shard_map/pallas_call | solution.py:140
  81.1 1.3 reshape.891
  82.3 2.4 %copy.52 = f32[2,2,16,9,8,8]{2,1,0,5,4,3:T(2,128)} copy(f32[2,2,16,9,8,8]{4,2,1,3,5,0:T(8,128)S(1)} %bitcast.147) | data formatting | bytes 294912 | tf_op jit(solution)/shard_map/transpose | solution.py:206
  84.7 2.2 reshape.892
  86.9 1.0 copy.53
  87.9 1.3 reshape.893
  89.2 2.2 copy.54
  91.4 2.2 reshape.894
  93.5 1.0 copy.55
  94.7 4.1 %all-to-all-start.1 = ((bf16[8,32,1024]{2,1,0:T(8,128)(2,1)}), bf16[8,32,1024]{2,1,0:T(8,128)(2,1)S(1)}, u32[]{:S(2)}, u32[]{:S(2)}) async-start(bf16[8,32,1024]{2,1,0:T(8,128)(2,1)} %bitcast.45), calls=%async_computation.1 | async-start | bytes 1048576 | tf_op jit(solution)/shard_map/all_to_all | solution.py:238
  98.8 128.5 %all-reduce.19.cloned.1.call-done = (f32[9,8,8,64]{3,0,2,1:T(8,128)}, f32[9,8,8,64]{3,0,2,1:T(8,128)}) async-done(((f32[9,8,8,64]{3,0,2,1:T(8,128)}, f32[9,8,8,64]{3,0,2,1:T(8,128)}), (f32[9,8,8,64]{3,0,2,1:T(8,128)}, f32[9,8,8,64]{3,0,2,1:T(8,128)})) %all-reduce.19.cloned.1.call-update) | async-done | bytes 294928 | tf_op jit(solution)/shard_map/psum | solution.py:241
  227.3 1.5 convolution_multiply_fusion.1
  228.8 0.8 copy.56
  229.6 0.4 convolution_multiply_fusion
  230.0 0.8 copy.57
  231.1 0.6 copy.84
  231.8 1.0 reshape.890
  (48 shorter events, 2.0 us)
Async XLA Ops:
  7.2 12.0 %copy-start.5 = (pred[128]{0:T(512)(128)(4,1)S(1)}, pred[128]{0:T(512)(128)(4,1)}, u32[]{:S(2)}) copy-start(pred[128]{0:T(512)(128)(4,1)} %constant.293.clone.1) | copy-start | bytes 388
  7.9 8.0 %copy-start.4 = (f32[8,512]{1,0:T(8,128)}, f32[8,512]{1,0:T(8,128)S(1)}, u32[]{:S(2)}) copy-start(f32[8,512]{1,0:T(8,128)S(1)} %subtract_convert_fusion) | copy-start | bytes 49156
  8.5 46.9 %collective-permute-start.1 = (f32[1,512]{1,0:T(1,128)}, f32[1,512]{1,0:T(1,128)}, u32[]{:S(2)}, u32[]{:S(2)}) collective-permute-start(f32[1,512]{1,0:T(1,128)} %get-tuple-element.40), channel_id=1, source_target_pairs={{1,0},{2,1},{3,2},{5,4},{6,5},{7,6},{9,8},{10,9},{11,10},{13,12},{... | collective-permute-start | bytes 6152 | tf_op jit(solution)/shard_map/ppermute | solution.py:178
  9.8 45.6 %collective-permute-start = (f32[1,512]{1,0:T(1,128)}, f32[1,512]{1,0:T(1,128)}, u32[]{:S(2)}, u32[]{:S(2)}) collective-permute-start(f32[1,512]{1,0:T(1,128)} %get-tuple-element.39), channel_id=1, source_target_pairs={{0,1},{1,2},{2,3},{4,5},{5,6},{6,7},{8,9},{9,10},{10,11},{12,13},{... | collective-permute-start | bytes 6152 | tf_op jit(solution)/shard_map/ppermute | solution.py:177
  19.9 13.2 %copy-start = (bf16[32,9,8,8]{0,3,2,1:T(8,128)(2,1)S(1)}, bf16[32,9,8,8]{0,3,2,1:T(8,128)(2,1)}, u32[]{:S(2)}) copy-start(bf16[32,9,8,8]{0,3,2,1:T(8,128)(2,1)} %param.11) | copy-start | bytes 110596
  24.6 32.4 %all-to-all-start = ((bf16[8,2,32,8,128]{4,3,2,1,0:T(8,128)(2,1)}), bf16[8,2,32,8,128]{4,3,2,1,0:T(8,128)(2,1)S(1)}, u32[]{:S(2)}, u32[]{:S(2)}) async-start(bf16[8,2,32,8,128]{4,3,2,1,0:T(8,128)(2,1)} %bitcast_dynamic-update-slice_fusion), calls=%async_computation | async-start | bytes 2097152 | tf_op jit(solution)/shard_map/all_to_all | solution.py:230
  28.8 198.5 %all-reduce.19.cloned.1.call-start = ((), (), s32[]{:S(2)}) async-start(), calls=%async_computation.2 | async-start | bytes 2097152 | tf_op jit(solution)/shard_map/psum | solution.py:241
  44.1 2.0 copy-start.3
  50.0 3.6 %copy-start.1 = (f32[2,8,2304]{2,1,0:T(8,128)S(1)}, f32[2,8,2304]{2,1,0:T(8,128)}, u32[]{:S(2)}) copy-start(f32[2,8,2304]{2,1,0:T(8,128)} %reshape.885) | copy-start | bytes 442372
  57.4 12.1 %collective-permute-start.5 = (bf16[8,32,1,128]{3,2,1,0:T(2,128)(2,1)S(1)}, bf16[8,32,1,128]{3,2,1,0:T(2,128)(2,1)S(1)}, u32[]{:S(2)}, u32[]{:S(2)}) collective-permute-start(bf16[8,32,1,128]{3,2,1,0:T(2,128)(2,1)S(1)} %get-tuple-element.23), channel_id=1, source_target_pairs={{1,0},{2,1},{3,2},{5,4},{6,5},{7,6},{9,8},{10,9},{11,10},{13,12},{... | collective-permute-start | bytes 196616 | tf_op jit(solution)/shard_map/ppermute | solution.py:178
  58.7 10.9 %collective-permute-start.4 = (bf16[8,32,1,128]{3,2,1,0:T(2,128)(2,1)S(1)}, bf16[8,32,1,128]{3,2,1,0:T(2,128)(2,1)S(1)}, u32[]{:S(2)}, u32[]{:S(2)}) collective-permute-start(bf16[8,32,1,128]{3,2,1,0:T(2,128)(2,1)S(1)} %get-tuple-element.22), channel_id=1, source_target_pairs={{0,1},{1,2},{2,3},{4,5},{5,6},{6,7},{8,9},{9,10},{10,11},{12,13},{... | collective-permute-start | bytes 196616 | tf_op jit(solution)/shard_map/ppermute | solution.py:177
  63.5 7.2 %collective-permute-start.3 = (bf16[8,32,2,128]{3,2,1,0:T(2,128)(2,1)S(1)}, bf16[8,32,2,128]{3,2,1,0:T(2,128)(2,1)S(1)}, u32[]{:S(2)}, u32[]{:S(2)}) collective-permute-start(bf16[8,32,2,128]{3,2,1,0:T(2,128)(2,1)S(1)} %get-tuple-element.25), channel_id=1, source_target_pairs={{1,0},{2,1},{3,2},{5,4},{6,5},{7,6},{9,8},{10,9},{11,10},{13,12},{... | collective-permute-start | bytes 393224 | tf_op jit(solution)/shard_map/ppermute | solution.py:178
  64.8 7.1 %collective-permute-start.2 = (bf16[8,32,2,128]{3,2,1,0:T(2,128)(2,1)S(1)}, bf16[8,32,2,128]{3,2,1,0:T(2,128)(2,1)S(1)}, u32[]{:S(2)}, u32[]{:S(2)}) collective-permute-start(bf16[8,32,2,128]{3,2,1,0:T(2,128)(2,1)S(1)} %get-tuple-element.24), channel_id=1, source_target_pairs={{0,1},{1,2},{2,3},{4,5},{5,6},{6,7},{8,9},{9,10},{10,11},{12,13},{... | collective-permute-start | bytes 393224 | tf_op jit(solution)/shard_map/ppermute | solution.py:177
  94.7 136.1 %all-to-all-start.1 = ((bf16[8,32,1024]{2,1,0:T(8,128)(2,1)}), bf16[8,32,1024]{2,1,0:T(8,128)(2,1)S(1)}, u32[]{:S(2)}, u32[]{:S(2)}) async-start(bf16[8,32,1024]{2,1,0:T(8,128)(2,1)} %bitcast.45), calls=%async_computation.1 | async-start | bytes 1048576 | tf_op jit(solution)/shard_map/all_to_all | solution.py:238
  227.3 2.3 copy-start.2
Sparse Core Ops, SparseCore 0:
  94.7 132.6 all-reduce.18

commit v2 on v1

v2 whole, which is shorter than its diff:
```python
import functools
import math

import jax
import jax.numpy as jnp
from jax import lax
from jax.experimental import pallas as pl
from jax.experimental.pallas import tpu as pltpu
from jax.sharding import PartitionSpec as P

G = 32
HALF = 16
LANES = 128
BF16 = jnp.bfloat16
F32 = jnp.float32


def split_element(sector):
    return sector % HALF, sector // HALF


def selection(rot, ref, mirrored):
    p = lax.broadcasted_iota(jnp.int32, (256, 256), 0)
    q = lax.broadcasted_iota(jnp.int32, (256, 256), 1)
    h = q >> 3
    turned = (rot + (1 - 2 * ref) * (h & 15)) & 15
    side = (ref + (h >> 4)) & 1
    if mirrored:
        turned = (-turned) & 15
        side = 1 - side
    wanted = ((side * HALF + turned) << 3) + (q & 7)
    return jnp.where(p == wanted, 1.0, 0.0).astype(BF16)


def bank_rows(bank, out):
    c = lax.broadcasted_iota(jnp.int32, (8, 256), 0)
    q = lax.broadcasted_iota(jnp.int32, (8, 256), 1)
    spread = jnp.where(c == (q & 7), 1.0, 0.0).astype(BF16)
    lane = lax.broadcasted_iota(jnp.int32, (72, 256), 1) >> 3
    total = jnp.zeros((72, 256), F32)
    for e in range(G):
        wide = dot(bank[e * 72 : (e + 1) * 72, :], spread)
        total = jnp.where(lane == e, wide, total)
    out[...] = total.astype(BF16)


def build_weights(rows, picks, dst, base_ref, flip):
    for s in range(2):
        base_ref[...] = dot(rows[...], picks[s])
        for k in range(9):
            for m in range(2):
                at = k * 256 + m * LANES
                base = base_ref[8 * k : 8 * k + 8, m * LANES : (m + 1) * LANES]
                turned = [base if r == 0 else pltpu.roll(base, 8 * r, 1) for r in range(HALF)]
                if flip is not None:
                    turned = [jnp.where(flip, turned[-r % HALF], turned[r]) for r in range(HALF)]
                for r in range(0, HALF, 2):
                    both = jnp.concatenate([turned[r], turned[r + 1]], axis=0).astype(BF16)
                    row = (s * HALF + r) * 8
                    dst[row : row + 16, at : at + LANES] = both


def fold(product, folded, tap_row, flip):
    for sg in range(2):
        for b in range(3):
            for m in range(2):
                lane = slice(b * 256 + m * LANES, b * 256 + (m + 1) * LANES)
                total = None
                for r in range(HALF):
                    row = (sg * HALF + r) * 8
                    piece = product[row : row + 8, lane]
                    if r > 0:
                        back = pltpu.roll(piece, LANES - 8 * r, 1)
                        if flip is not None:
                            back = jnp.where(flip, pltpu.roll(piece, 8 * r, 1), back)
                        piece = back
                    total = piece if total is None else total + piece
                at = (tap_row * 3 + b) * 8
                folded[sg, at : at + 8, m * LANES : (m + 1) * LANES] = total


def unselect(folded, picks):
    total = None
    for s in range(2):
        rest = folded[s]
        for _ in range(3):
            part = rest.astype(BF16)
            rest = rest - part.astype(F32)
            term = dot_nt(part, picks[s])
            total = term if total is None else total + term
    return total


def shifted(value, by):
    if by == 0:
        return value
    return pltpu.roll(value.astype(F32), by % LANES, 1).astype(BF16)


def stack_shifts(src, dst, first, count, sign):
    for i in range(first, first + count):
        cols = slice(i * LANES, (i + 1) * LANES)
        value = src[:, cols]
        for b in range(3):
            dst[b * 256 : (b + 1) * 256, cols] = shifted(value, sign * (1 - b))


def dot(a, b):
    return jnp.dot(a, b, preferred_element_type=F32)


def dot_nt(a, b):
    return lax.dot_general(a, b, (((1,), (1,)), ((), ())), preferred_element_type=F32)


def compute(width, sector, bank1, bank2, opened, x, cot, wake, shares, w1, w2, w2t, xs, hs, cs, dfac, hid, own, prod, rows, base, pick, folded):
    rot, ref = split_element(sector[0])
    flip = (lax.broadcasted_iota(jnp.int32, (8, LANES), 0) * 0 + ref) == 1
    for s in range(2):
        pick[s] = selection(rot, ref, s == 1)
        pick[2 + s] = selection(0, 0, s == 1)
    bank_rows(bank1, rows)
    build_weights(rows, [pick[0], pick[1]], w1, base, flip)
    bank_rows(bank2, rows)
    build_weights(rows, [pick[2], pick[3]], w2, base, None)
    for k in range(9):
        cols = slice(k * 256, (k + 1) * 256)
        w2t[:, cols] = dot_nt(pick[2], w2[:, cols]).astype(BF16)
    lane = lax.broadcasted_iota(jnp.int32, (256, LANES), 1)
    inner = (lane >= 2) & (lane < 2 + width)
    stack_shifts(x, xs, 0, 12, 1)
    for n in range(5):
        total = sum(
            dot(w1[:, a * 768 : (a + 1) * 768], xs[:, (2 * n + a) * LANES : (2 * n + a + 2) * LANES])
            for a in range(3)
        )
        cols = slice(2 * n * LANES, (2 * n + 2) * LANES)
        free = opened[0:1, cols]
        sig = jax.nn.sigmoid(total)
        hid[:, cols] = (total * sig * free).astype(BF16)
        dfac[:, cols] = free * sig * (1.0 + total * (1.0 - sig))
    stack_shifts(hid, hs, 0, 10, 1)
    for n in range(4):
        total = sum(
            dot(w2[:, a * 768 : (a + 1) * 768], hs[:, (2 * n + a) * LANES : (2 * n + a + 2) * LANES])
            for a in range(3)
        )
        wake[:, 2 * n * LANES : (2 * n + 2) * LANES] = total.astype(BF16)
    stack_shifts(cot, cs, 0, 10, -1)
    for i in range(8):
        value = cot[:, (i + 1) * LANES : (i + 2) * LANES].astype(F32)
        own[:, i * LANES : (i + 1) * LANES] = jnp.where(inner, value, 0.0).astype(BF16)
    for a in range(3):
        prod[...] = dot_nt(own[...], hs[:, a * LANES : (a + 8) * LANES])
        fold(prod, folded, a, None)
    shares[72:144, :] = unselect(folded, [pick[2], pick[3]])
    for n in range(4):
        total = sum(
            dot(
                w2t[:, a * 768 : (a + 1) * 768],
                cs[:, (2 * n + 2 - a) * LANES : (2 * n + 4 - a) * LANES],
            )
            for a in range(3)
        )
        cols = slice((2 * n + 1) * LANES, (2 * n + 3) * LANES)
        total = total * dfac[:, cols]
        for i in range(2):
            value = jnp.where(inner, total[:, i * LANES : (i + 1) * LANES], 0.0)
            own[:, (2 * n + i) * LANES : (2 * n + i + 1) * LANES] = value.astype(BF16)
    for a in range(3):
        prod[...] = dot_nt(own[...], xs[:, (a + 1) * LANES : (a + 9) * LANES])
        fold(prod, folded, a, flip)
    shares[0:72, :] = unselect(folded, [pick[0], pick[1]])


def expand(scale, shares, one, two):
    for layer, out in enumerate((one, two)):
        value = shares[layer * 72 : (layer + 1) * 72, :] * scale
        for e in range(G):
            out[e * 72 : (e + 1) * 72, :] = value[:, e * 8 : e * 8 + 8]


def expand_kernel(scale, shares):
    vmem = pl.BlockSpec(memory_space=pltpu.VMEM)
    out = jax.ShapeDtypeStruct((G * 72, 8), F32)
    return pl.pallas_call(
        functools.partial(expand, scale),
        out_shape=(out, out),
        in_specs=[vmem],
        out_specs=(vmem, vmem),
        compiler_params=pltpu.CompilerParams(vmem_limit_bytes=32 * 1024 * 1024),
    )(shares)


def pack(width, x, cot, out, wide):
    local, height, extent = x.shape
    phases = LANES // width
    for which, src in enumerate((x, cot)):
        wide[...] = src[...].astype(F32)
        for r in range(height):
            row = jnp.concatenate([wide[:, r, :], jnp.zeros((local, LANES), F32)], axis=1)
            for phase in range(phases):
                moved = pltpu.roll(row, (2 - width * phase) % (extent + LANES), 1).astype(BF16)
                for m in range(extent // LANES):
                    piece = moved[:, m * LANES : (m + 1) * LANES]
                    out[m * phases + phase, which, :, r * LANES : (r + 1) * LANES] = piece


def pack_kernel(width, x, cot):
    local, height, extent = x.shape
    vmem = pl.BlockSpec(memory_space=pltpu.VMEM)
    return pl.pallas_call(
        functools.partial(pack, width),
        out_shape=jax.ShapeDtypeStruct((extent // width, 2, local, height * LANES), BF16),
        in_specs=[vmem] * 2,
        out_specs=vmem,
        scratch_shapes=[pltpu.VMEM((local, height, extent), F32)],
        compiler_params=pltpu.CompilerParams(vmem_limit_bytes=32 * 1024 * 1024),
    )(x, cot)


def local_kernel(width, sector, bank1, bank2, opened, x, cot):
    vmem = pl.BlockSpec(memory_space=pltpu.VMEM)
    smem = pl.BlockSpec(memory_space=pltpu.SMEM)
    return pl.pallas_call(
        functools.partial(compute, width),
        out_shape=(
            jax.ShapeDtypeStruct((256, 8 * LANES), BF16),
            jax.ShapeDtypeStruct((144, 256), F32),
        ),
        in_specs=[smem] + [vmem] * 5,
        out_specs=(vmem,) * 2,
        scratch_shapes=[
            pltpu.VMEM((256, 2304), BF16),
            pltpu.VMEM((256, 2304), BF16),
            pltpu.VMEM((256, 2304), BF16),
            pltpu.VMEM((768, 12 * LANES), BF16),
            pltpu.VMEM((768, 10 * LANES), BF16),
            pltpu.VMEM((768, 10 * LANES), BF16),
            pltpu.VMEM((256, 10 * LANES), F32),
            pltpu.VMEM((256, 10 * LANES), BF16),
            pltpu.VMEM((256, 8 * LANES), BF16),
            pltpu.VMEM((256, 768), F32),
            pltpu.VMEM((72, 256), BF16),
            pltpu.VMEM((72, 256), F32),
            pltpu.VMEM((4, 256, 256), BF16),
            pltpu.VMEM((2, 72, 256), F32),
        ],
        compiler_params=pltpu.CompilerParams(vmem_limit_bytes=48 * 1024 * 1024),
    )(sector, bank1, bank2, opened, x, cot)


def edges(rows, width):
    count = lax.axis_size("strip")
    height = rows.shape[-2]
    up = [(i, i + 1) for i in range(count - 1)]
    down = [(i + 1, i) for i in range(count - 1)]
    before = lax.ppermute(rows[..., height - width :, :], "strip", up)
    after = lax.ppermute(rows[..., :width, :], "strip", down)
    return jnp.concatenate([before, rows, after], axis=-2)


def summed(shares):
    axes = ("orient", "strip")
    count = lax.axis_size("orient") * lax.axis_size("strip")
    parts = lax.all_to_all(shares.reshape(count, -1), axes, 0, 0, tiled=True)
    part = jnp.broadcast_to(jnp.sum(parts, axis=0, keepdims=True), parts.shape)
    return lax.all_to_all(part, axes, 0, 0, tiled=True).reshape(shares.shape)


def shards(inflow_field, kernel_one, kernel_two, turbine_mask, wind_sector, wake_cotangent):
    groups, channels, height, extent = inflow_field.shape
    local = groups * channels
    devices = lax.axis_size("orient")
    width = extent // devices
    scale = 1.0 / math.sqrt(G * height * lax.axis_size("strip") * extent)
    shape = (local, height, extent)
    packed = pack_kernel(width, inflow_field.reshape(shape), wake_cotangent.reshape(shape))
    free = jnp.pad((1 - turbine_mask).astype(F32), ((0, 0), (2, LANES)))
    free = lax.dynamic_slice_in_dim(free, lax.axis_index("orient") * width, LANES, axis=1)
    free = jnp.where(jnp.arange(LANES) < width + 4, free, 0.0)
    free = edges(free, 1)
    opened = jnp.broadcast_to(free.reshape(1, -1), (8, (height + 2) * LANES))
    spread = lax.all_to_all(packed, "orient", 0, 0, tiled=True)
    spread = spread.reshape(devices, 2, local, height, LANES)
    x = edges(spread[:, 0], 2).reshape(devices * local, -1)
    cot = edges(spread[:, 1], 1).reshape(devices * local, -1)
    bank1, bank2 = kernel_one.reshape(-1, channels), kernel_two.reshape(-1, channels)
    wake, shares = local_kernel(width, wind_sector, bank1, bank2, opened, x, cot)
    wake = lax.all_to_all(wake.reshape(devices, local, -1), "orient", 0, 0, tiled=True)
    wake = wake.reshape(devices, local, height, LANES)[..., 2 : 2 + extent // devices]
    wake = wake.transpose(1, 2, 0, 3).reshape(groups, channels, height, extent)
    one, two = expand_kernel(scale, summed(shares))
    return (wake, one.reshape(kernel_one.shape), two.reshape(kernel_two.shape))


def solution(mesh):
    return jax.shard_map(
        shards,
        mesh=mesh,
        in_specs=(
            P("orient", None, "strip", None),
            P(),
            P(),
            P("strip", None),
            P(),
            P("orient", None, "strip", None),
        ),
        out_specs=(P("orient", None, "strip", None), P(), P()),
        check_vma=False,
    )
```

time: 240 us -> 93.3 us (0.39)
  waiting for transfers between devices: 130 us -> 29.6 us
  local copies, waits for them, and re-layouts: 35.2 us -> 8.93 us
  other arithmetic: 16.7 us -> 1.81 us
  between operations: 15 us -> 1.55 us
  blocking collectives: 0 us -> 11.4 us
  matrix products: 6.68 us -> 0 us
  Pallas kernels: 8.36 us -> 12.4 us
    psum x1 -> x0, waiting for transfers between devices: 129 us -> none  [shards(): t1, t2 = lax.psum((t1, t2), ('orient', 'strip'))]
    reshape x7 -> x1, local copies, waits for them, and re-layouts: 12.8 us -> 0.04 us  [summed(): return lax.all_to_all(part, axes, 0, 0, tiled=True).reshape(shares.shape)]
    all_to_all x0 -> x1, blocking collectives: none -> 11.4 us  [summed(): parts = lax.all_to_all(shares.reshape(count, -1), axes, 0, 0, tiled=True)]
    transpose x5 -> x0, local copies, waits for them, and re-layouts: 10.2 us -> none  [the longest x3 5.62 us: turned_bank(): return picked.transpose(order).reshape(2, 8, 2304)]
    all_to_all x1, waiting for transfers between devices: 0.01 us -> 9.57 us  [shards(): lax.all_to_all(wake.reshape(devices, local, -1), 'orient', 0, 0, tiled=True)]
    ppermute x3, waiting for transfers between devices: 0.28 us -> 7.02 us  [edges(): after = lax.ppermute(rows[..., :width, :], 'strip', down)]
    dot_general x5 -> x0, matrix products: 6.68 us -> none  [the longest x3 4.84 us: turned_bank(): picked = jnp.dot(onehot, bank.reshape(G, -1), preferred_element_type=F32)]
    all_to_all x0 -> x1, waiting for transfers between devices: none -> 6.45 us  [summed(): return lax.all_to_all(part, axes, 0, 0, tiled=True).reshape(shares.shape)]
  transfers between devices with their start and end apart: 9 -> 9, of which waited for: 3 -> 6; matrix products, arithmetic and copies ran while one was open for 17% -> 4% of each run, Pallas kernels for 0% -> 0%
where the time goes in v2:
time: 93.3 us; the launch traced here: 92.8 us
  waiting for transfers between devices  29.6 us (32%)
  starting transfers between devices  27.2 us (29%)
  Pallas kernels  12.4 us (13%)
  blocking collectives  11.4 us (12%)
  local copies, waits for them, and re-layouts  8.93 us (10%)
  other arithmetic  1.81 us (2%)
  between operations  1.55 us (2%)
    ppermute x3, starting transfers between devices, edges(): before = lax.ppermute(rows[..., height - width:, :], 'strip', up)  11.5 us
    all_to_all x1, blocking collectives, summed(): parts = lax.all_to_all(shares.reshape(count, -1), axes, 0, 0, tiled=True)  11.4 us
    pallas_call x1, Pallas kernels, local_kernel(): pl.pallas_call(functools.partial(compute, width), out_shape=(jax.ShapeDty...  10.2 us
    all_to_all x1, waiting for transfers between devices, shards(): lax.all_to_all(wake.reshape(devices, local, -1), 'orient', 0, 0, tiled=True)  9.57 us
    ppermute x3, waiting for transfers between devices, edges(): after = lax.ppermute(rows[..., :width, :], 'strip', down)  7.02 us
    all_to_all x1, waiting for transfers between devices, summed(): return lax.all_to_all(part, axes, 0, 0, tiled=True).reshape(shares.shape)  6.45 us
    all_to_all x1, waiting for transfers between devices, shards(): spread = lax.all_to_all(packed, 'orient', 0, 0, tiled=True)  6.37 us
    unnamed x19, local copies, waits for them, and re-layouts  6.22 us
  transfers between devices with their start and end apart: 9, of which 6 were waited for; matrix products, arithmetic and copies ran while one was open for 4% of the time, Pallas kernels for 0%

profile of v2, /device:TPU:0, one launch (start us, length us, event | category | flops | bytes accessed | tf_op | source)
XLA Modules:
  0.0 92.8 jit_solution(2783649718324322868)
XLA Ops:
  0.6 0.0 copy-start
  0.6 0.9 %copy-done = bf16[4,8,8,512]{3,2,1,0:T(8,128)(2,1)S(1)} copy-done((bf16[4,8,8,512]{3,2,1,0:T(8,128)(2,1)S(1)}, bf16[4,8,8,512]{3,2,1,0:T(8,128)(2,1)}, u32[]{:S(2)}) %copy-start) | copy-done | bytes 262168
  1.6 0.0 copy-start.1
  1.6 0.9 %copy-done.1 = bf16[4,8,8,512]{3,2,1,0:T(8,128)(2,1)S(1)} copy-done((bf16[4,8,8,512]{3,2,1,0:T(8,128)(2,1)S(1)}, bf16[4,8,8,512]{3,2,1,0:T(8,128)(2,1)}, u32[]{:S(2)}) %copy-start.1) | copy-done | bytes 262168
  2.5 1.5 %shard_map.85 = bf16[8,2,32,1024]{3,2,1,0:T(8,128)(2,1)} custom-call(bf16[32,8,512]{2,1,0:T(8,128)(2,1)S(1)} %bitcast.47, bf16[32,8,512]{2,1,0:T(8,128)(2,1)S(1)} %bitcast.48), custom_call_target="tpu_custom_call" | custom-call | tf_op jit(solution)/shard_map/pallas_call | solution.py:212
  4.1 0.0 copy-start.4
  4.1 0.0 copy-start.2
  4.1 0.0 copy-start.3
  4.1 5.3 %all-to-all-start = ((bf16[8,2,32,1024]{3,2,1,0:T(8,128)(2,1)}), bf16[8,2,32,1024]{3,2,1,0:T(8,128)(2,1)S(1)}, u32[]{:S(2)}, u32[]{:S(2)}) async-start(bf16[8,2,32,1024]{3,2,1,0:T(8,128)(2,1)} %shard_map.85), calls=%async_computation | async-start | bytes 2097152 | tf_op jit(solution)/shard_map/all_to_all | solution.py:284
  9.4 0.0 copy-done.4
  9.4 0.1 fusion
  9.5 3.5 %collective-permute-start = (f32[1,128]{1,0:T(1,128)S(1)}, f32[1,128]{1,0:T(1,128)S(1)}, u32[]{:S(2)}, u32[]{:S(2)}) collective-permute-start(f32[1,128]{1,0:T(1,128)S(1)} %get-tuple-element.26), channel_id=1, source_target_pairs={{0,1},{1,2},{2,3},{4,5},{5,6},{6,7},{8,9},{9,10},{10,11},{12,13},{... | collective-permute-start | bytes 1544 | tf_op jit(solution)/shard_map/ppermute | solution.py:258
  13.0 1.3 %collective-permute-start.1 = (f32[1,128]{1,0:T(1,128)S(1)}, f32[1,128]{1,0:T(1,128)S(1)}, u32[]{:S(2)}, u32[]{:S(2)}) collective-permute-start(f32[1,128]{1,0:T(1,128)S(1)} %get-tuple-element.27), channel_id=1, source_target_pairs={{1,0},{2,1},{3,2},{5,4},{6,5},{7,6},{9,8},{10,9},{11,10},{13,12},{... | collective-permute-start | bytes 1544 | tf_op jit(solution)/shard_map/ppermute | solution.py:259
  14.3 0.0 copy-done.2
  14.3 0.4 copy.23
  14.7 0.0 copy-done.3
  14.7 0.4 copy.24
  15.7 0.0 collective-permute-done
  15.7 2.7 %collective-permute-done.1 = f32[1,128]{1,0:T(1,128)S(1)} collective-permute-done((f32[1,128]{1,0:T(1,128)S(1)}, f32[1,128]{1,0:T(1,128)S(1)}, u32[]{:S(2)}, u32[]{:S(2)}) %collective-permute-start.1) | collective-permute-done | bytes 544 | tf_op jit(solution)/shard_map/ppermute | solution.py:259
  18.4 6.4 %all-to-all-done = bf16[8,2,32,1024]{3,2,1,0:T(8,128)(2,1)S(1)} async-done(((bf16[8,2,32,1024]{3,2,1,0:T(8,128)(2,1)}), bf16[8,2,32,1024]{3,2,1,0:T(8,128)(2,1)S(1)}, u32[]{:S(2)}, u32[]{:S(2)}) %all-to-all-start) | async-done | bytes 1048608 | tf_op jit(solution)/shard_map/all_to_all | solution.py:284
  24.8 0.3 copy.34
  25.1 0.1 slice_bitcast_fusion
  25.1 0.2 fusion.1
  25.4 3.5 %collective-permute-start.4 = (bf16[8,32,1,128]{3,2,1,0:T(2,128)(2,1)S(1)}, bf16[8,32,1,128]{3,2,1,0:T(2,128)(2,1)S(1)}, u32[]{:S(2)}, u32[]{:S(2)}) collective-permute-start(bf16[8,32,1,128]{3,2,1,0:T(2,128)(2,1)S(1)} %get-tuple-element.22), channel_id=1, source_target_pairs={{0,1},{1,2},{2,3},{4,5},{5,6},{6,7},{8,9},{9,10},{10,11},{12,13},{... | collective-permute-start | bytes 196616 | tf_op jit(solution)/shard_map/ppermute | solution.py:258
  28.9 1.3 %collective-permute-start.5 = (bf16[8,32,1,128]{3,2,1,0:T(2,128)(2,1)S(1)}, bf16[8,32,1,128]{3,2,1,0:T(2,128)(2,1)S(1)}, u32[]{:S(2)}, u32[]{:S(2)}) collective-permute-start(bf16[8,32,1,128]{3,2,1,0:T(2,128)(2,1)S(1)} %get-tuple-element.23), channel_id=1, source_target_pairs={{1,0},{2,1},{3,2},{5,4},{6,5},{7,6},{9,8},{10,9},{11,10},{13,12},{... | collective-permute-start | bytes 196616 | tf_op jit(solution)/shard_map/ppermute | solution.py:259
  30.2 0.2 fusion.2
  30.4 4.6 %collective-permute-start.2 = (bf16[8,32,2,128]{3,2,1,0:T(2,128)(2,1)S(1)}, bf16[8,32,2,128]{3,2,1,0:T(2,128)(2,1)S(1)}, u32[]{:S(2)}, u32[]{:S(2)}) collective-permute-start(bf16[8,32,2,128]{3,2,1,0:T(2,128)(2,1)S(1)} %get-tuple-element.24), channel_id=1, source_target_pairs={{0,1},{1,2},{2,3},{4,5},{5,6},{6,7},{8,9},{9,10},{10,11},{12,13},{... | collective-permute-start | bytes 393224 | tf_op jit(solution)/shard_map/ppermute | solution.py:258
  35.0 1.5 %collective-permute-start.3 = (bf16[8,32,2,128]{3,2,1,0:T(2,128)(2,1)S(1)}, bf16[8,32,2,128]{3,2,1,0:T(2,128)(2,1)S(1)}, u32[]{:S(2)}, u32[]{:S(2)}) collective-permute-start(bf16[8,32,2,128]{3,2,1,0:T(2,128)(2,1)S(1)} %get-tuple-element.25), channel_id=1, source_target_pairs={{1,0},{2,1},{3,2},{5,4},{6,5},{7,6},{9,8},{10,9},{11,10},{13,12},{... | collective-permute-start | bytes 393224 | tf_op jit(solution)/shard_map/ppermute | solution.py:259
  36.5 0.0 collective-permute-done.4
  36.5 0.0 collective-permute-done.5
  36.5 0.7 pad_maximum_fusion.1
  37.1 0.2 copy.42
  37.3 0.1 collective-permute-done.2
  37.5 4.4 %collective-permute-done.3 = bf16[8,32,2,128]{3,2,1,0:T(2,128)(2,1)S(1)} collective-permute-done((bf16[8,32,2,128]{3,2,1,0:T(2,128)(2,1)S(1)}, bf16[8,32,2,128]{3,2,1,0:T(2,128)(2,1)S(1)}, u32[]{:S(2)}, u32[]{:S(2)}) %collective-permute-start.3) | collective-permute-done | bytes 131104 | tf_op jit(solution)/shard_map/ppermute | solution.py:259
  41.8 0.6 pad_maximum_fusion
  42.4 0.2 copy.41
  42.7 10.2 %shard_map.86 = (bf16[256,1024]{1,0:T(8,128)(2,1)}, f32[144,256]{1,0:T(8,128)S(1)}) custom-call(s32[1]{0:T(128)S(6)} %copy.44.sector, bf16[2304,8]{1,0:T(8,128)(2,1)S(1)} %bitcast.43, bf16[2304,8]{1,0:T(8,128)(2,1)S(1)} %bitcast.44, f32[8,1280]{1,0:T(8,128)S(1)} %broadcast_in_dim.24.opened, bf16[256,1536]{1,0:T(8,128)(2,1)S(1)} %bitcast.41, ...), custom_call_target="tpu_custom_call" | custom-call | tf_op jit(solution)/shard_map/pallas_call | solution.py:225
  52.9 0.1 all_to_all.21
  53.0 11.4 %all_to_all.26 = f32[32,1,1152]{2,1,0:T(1,128)S(1)} all-to-all(f32[32,1,1152]{2,1,0:T(1,128)S(1)} %all_to_all.21), channel_id=1, replica_groups=mesh['orient'=8,'strip'=4] {'orient','strip'}, dimensions={0} | all-to-all | bytes 294912 | tf_op jit(solution)/shard_map/all_to_all | solution.py:266
  64.5 3.5 %all-to-all-start.1 = ((bf16[8,32,1024]{2,1,0:T(8,128)(2,1)}), bf16[8,32,1024]{2,1,0:T(8,128)(2,1)S(1)}, u32[]{:S(2)}, u32[]{:S(2)}) async-start(bf16[8,32,1024]{2,1,0:T(8,128)(2,1)} %bitcast.7), calls=%async_computation.1 | async-start | bytes 1048576 | tf_op jit(solution)/shard_map/all_to_all | solution.py:290
  68.0 0.1 reduce_sum.9
  68.1 9.6 %all-to-all-done.1 = bf16[8,32,1024]{2,1,0:T(8,128)(2,1)S(1)} async-done(((bf16[8,32,1024]{2,1,0:T(8,128)(2,1)}), bf16[8,32,1024]{2,1,0:T(8,128)(2,1)S(1)}, u32[]{:S(2)}, u32[]{:S(2)}) %all-to-all-start.1) | async-done | bytes 524320 | tf_op jit(solution)/shard_map/all_to_all | solution.py:290
  77.6 0.7 broadcast_in_dim.25
  78.4 2.8 %all-to-all-start.3 = ((f32[32,1,1152]{2,1,0:T(1,128)}), f32[32,1,1152]{2,1,0:T(1,128)S(1)}, u32[]{:S(2)}, u32[]{:S(2)}) async-start(f32[32,1,1152]{2,1,0:T(1,128)} %broadcast_in_dim.25), calls=%async_computation.3 | async-start | bytes 294912 | tf_op jit(solution)/shard_map/all_to_all | solution.py:268
  81.2 0.1 copy.37
  81.3 0.2 slice.42
  81.5 0.6 copy.43
  82.1 1.0 %reshape.67 = bf16[4,8,8,512]{3,2,1,0:T(8,128)(2,1)} reshape(bf16[32,8,8,64]{3,2,1,0:T(8,128)(2,1)S(1)} %bitcast.55) | data formatting | bytes 524288 | tf_op jit(solution)/shard_map/reshape | solution.py:292
  83.1 6.5 %all-to-all-done.3 = f32[32,1,1152]{2,1,0:T(1,128)S(1)} async-done(((f32[32,1,1152]{2,1,0:T(1,128)}), f32[32,1,1152]{2,1,0:T(1,128)S(1)}, u32[]{:S(2)}, u32[]{:S(2)}) %all-to-all-start.3) | async-done | bytes 147488 | tf_op jit(solution)/shard_map/all_to_all | solution.py:268
  89.6 0.3 reduce.1
  90.0 0.6 shard_map.87
  90.6 1.1 %copy.29 = f32[32,9,8,8]{0,3,2,1:T(8,128)} copy(f32[32,9,8,8]{3,2,1,0:T(8,128)S(1)} %bitcast.46) | data formatting | bytes 147456
  91.7 1.1 %copy.30 = f32[32,9,8,8]{0,3,2,1:T(8,128)} copy(f32[32,9,8,8]{3,2,1,0:T(8,128)S(1)} %bitcast.45) | data formatting | bytes 147456
  (6 shorter events, 0.1 us)
Async XLA Ops:
  0.6 1.0 %copy-start = (bf16[4,8,8,512]{3,2,1,0:T(8,128)(2,1)S(1)}, bf16[4,8,8,512]{3,2,1,0:T(8,128)(2,1)}, u32[]{:S(2)}) copy-start(bf16[4,8,8,512]{3,2,1,0:T(8,128)(2,1)} %param.6) | copy-start | bytes 786436
  1.6 0.9 %copy-start.1 = (bf16[4,8,8,512]{3,2,1,0:T(8,128)(2,1)S(1)}, bf16[4,8,8,512]{3,2,1,0:T(8,128)(2,1)}, u32[]{:S(2)}) copy-start(bf16[4,8,8,512]{3,2,1,0:T(8,128)(2,1)} %param.11) | copy-start | bytes 786436
  4.1 5.3 %copy-start.4 = (s32[8,512]{1,0:T(8,128)S(1)}, s32[8,512]{1,0:T(8,128)}, u32[]{:S(2)}) copy-start(s32[8,512]{1,0:T(8,128)} %param.9) | copy-start | bytes 49156
  4.1 10.2 %copy-start.2 = (bf16[32,9,8,8]{0,3,2,1:T(8,128)(2,1)S(1)}, bf16[32,9,8,8]{0,3,2,1:T(8,128)(2,1)}, u32[]{:S(2)}) copy-start(bf16[32,9,8,8]{0,3,2,1:T(8,128)(2,1)} %param.7) | copy-start | bytes 110596
  4.1 10.6 %copy-start.3 = (bf16[32,9,8,8]{0,3,2,1:T(8,128)(2,1)S(1)}, bf16[32,9,8,8]{0,3,2,1:T(8,128)(2,1)}, u32[]{:S(2)}) copy-start(bf16[32,9,8,8]{0,3,2,1:T(8,128)(2,1)} %param.8) | copy-start | bytes 110596
  4.1 20.7 %all-to-all-start = ((bf16[8,2,32,1024]{3,2,1,0:T(8,128)(2,1)}), bf16[8,2,32,1024]{3,2,1,0:T(8,128)(2,1)S(1)}, u32[]{:S(2)}, u32[]{:S(2)}) async-start(bf16[8,2,32,1024]{3,2,1,0:T(8,128)(2,1)} %shard_map.85), calls=%async_computation | async-start | bytes 2097152 | tf_op jit(solution)/shard_map/all_to_all | solution.py:284
  9.5 6.2 %collective-permute-start = (f32[1,128]{1,0:T(1,128)S(1)}, f32[1,128]{1,0:T(1,128)S(1)}, u32[]{:S(2)}, u32[]{:S(2)}) collective-permute-start(f32[1,128]{1,0:T(1,128)S(1)} %get-tuple-element.26), channel_id=1, source_target_pairs={{0,1},{1,2},{2,3},{4,5},{5,6},{6,7},{8,9},{9,10},{10,11},{12,13},{... | collective-permute-start | bytes 1544 | tf_op jit(solution)/shard_map/ppermute | solution.py:258
  13.0 5.4 %collective-permute-start.1 = (f32[1,128]{1,0:T(1,128)S(1)}, f32[1,128]{1,0:T(1,128)S(1)}, u32[]{:S(2)}, u32[]{:S(2)}) collective-permute-start(f32[1,128]{1,0:T(1,128)S(1)} %get-tuple-element.27), channel_id=1, source_target_pairs={{1,0},{2,1},{3,2},{5,4},{6,5},{7,6},{9,8},{10,9},{11,10},{13,12},{... | collective-permute-start | bytes 1544 | tf_op jit(solution)/shard_map/ppermute | solution.py:259
  25.4 11.1 %collective-permute-start.4 = (bf16[8,32,1,128]{3,2,1,0:T(2,128)(2,1)S(1)}, bf16[8,32,1,128]{3,2,1,0:T(2,128)(2,1)S(1)}, u32[]{:S(2)}, u32[]{:S(2)}) collective-permute-start(bf16[8,32,1,128]{3,2,1,0:T(2,128)(2,1)S(1)} %get-tuple-element.22), channel_id=1, source_target_pairs={{0,1},{1,2},{2,3},{4,5},{5,6},{6,7},{8,9},{9,10},{10,11},{12,13},{... | collective-permute-start | bytes 196616 | tf_op jit(solution)/shard_map/ppermute | solution.py:258
  28.9 7.6 %collective-permute-start.5 = (bf16[8,32,1,128]{3,2,1,0:T(2,128)(2,1)S(1)}, bf16[8,32,1,128]{3,2,1,0:T(2,128)(2,1)S(1)}, u32[]{:S(2)}, u32[]{:S(2)}) collective-permute-start(bf16[8,32,1,128]{3,2,1,0:T(2,128)(2,1)S(1)} %get-tuple-element.23), channel_id=1, source_target_pairs={{1,0},{2,1},{3,2},{5,4},{6,5},{7,6},{9,8},{10,9},{11,10},{13,12},{... | collective-permute-start | bytes 196616 | tf_op jit(solution)/shard_map/ppermute | solution.py:259
  30.4 7.1 %collective-permute-start.2 = (bf16[8,32,2,128]{3,2,1,0:T(2,128)(2,1)S(1)}, bf16[8,32,2,128]{3,2,1,0:T(2,128)(2,1)S(1)}, u32[]{:S(2)}, u32[]{:S(2)}) collective-permute-start(bf16[8,32,2,128]{3,2,1,0:T(2,128)(2,1)S(1)} %get-tuple-element.24), channel_id=1, source_target_pairs={{0,1},{1,2},{2,3},{4,5},{5,6},{6,7},{8,9},{9,10},{10,11},{12,13},{... | collective-permute-start | bytes 393224 | tf_op jit(solution)/shard_map/ppermute | solution.py:258
  35.0 6.9 %collective-permute-start.3 = (bf16[8,32,2,128]{3,2,1,0:T(2,128)(2,1)S(1)}, bf16[8,32,2,128]{3,2,1,0:T(2,128)(2,1)S(1)}, u32[]{:S(2)}, u32[]{:S(2)}) collective-permute-start(bf16[8,32,2,128]{3,2,1,0:T(2,128)(2,1)S(1)} %get-tuple-element.25), channel_id=1, source_target_pairs={{1,0},{2,1},{3,2},{5,4},{6,5},{7,6},{9,8},{10,9},{11,10},{13,12},{... | collective-permute-start | bytes 393224 | tf_op jit(solution)/shard_map/ppermute | solution.py:259
  64.5 13.2 %all-to-all-start.1 = ((bf16[8,32,1024]{2,1,0:T(8,128)(2,1)}), bf16[8,32,1024]{2,1,0:T(8,128)(2,1)S(1)}, u32[]{:S(2)}, u32[]{:S(2)}) async-start(bf16[8,32,1024]{2,1,0:T(8,128)(2,1)} %bitcast.7), calls=%async_computation.1 | async-start | bytes 1048576 | tf_op jit(solution)/shard_map/all_to_all | solution.py:290
  78.4 11.2 %all-to-all-start.3 = ((f32[32,1,1152]{2,1,0:T(1,128)}), f32[32,1,1152]{2,1,0:T(1,128)S(1)}, u32[]{:S(2)}, u32[]{:S(2)}) async-start(f32[32,1,1152]{2,1,0:T(1,128)} %broadcast_in_dim.25), calls=%async_computation.3 | async-start | bytes 294912 | tf_op jit(solution)/shard_map/all_to_all | solution.py:268

commit v3 on v2

--- a/solution.py
+++ b/solution.py
@@ -250,22 +250,203 @@
     )(sector, bank1, bank2, opened, x, cot)
 
 
-def edges(rows, width):
-    count = lax.axis_size("strip")
-    height = rows.shape[-2]
-    up = [(i, i + 1) for i in range(count - 1)]
-    down = [(i + 1, i) for i in range(count - 1)]
-    before = lax.ppermute(rows[..., height - width :, :], "strip", up)
-    after = lax.ppermute(rows[..., :width, :], "strip", down)
-    return jnp.concatenate([before, rows, after], axis=-2)
-
-
-def summed(shares):
-    axes = ("orient", "strip")
-    count = lax.axis_size("orient") * lax.axis_size("strip")
-    parts = lax.all_to_all(shares.reshape(count, -1), axes, 0, 0, tiled=True)
-    part = jnp.broadcast_to(jnp.sum(parts, axis=0, keepdims=True), parts.shape)
-    return lax.all_to_all(part, axes, 0, 0, tiled=True).reshape(shares.shape)
+def remote(src, dst, send, recv, **to):
+    return pltpu.make_async_remote_copy(
+        src_ref=src,
+        dst_ref=dst,
+        send_sem=send,
+        recv_sem=recv,
+        device_id=to,
+        device_id_type=pl.DeviceIdType.MESH,
+    )
+
+
+def greet(**to):
+    barrier = pltpu.get_barrier_semaphore()
+    pl.semaphore_signal(barrier, inc=1, device_id=to, device_id_type=pl.DeviceIdType.MESH)
+
+
+def exchange_in(count, strips, packed, free, x, cot, opened, send, recv, edge_send, edge_recv):
+    me, z = lax.axis_index("orient"), lax.axis_index("strip")
+    for j in range(1, count):
+        greet(orient=lax.rem(me + j, count))
+    greet(strip=lax.rem(z + strips - 1, strips))
+    greet(strip=lax.rem(z + 1, strips))
+    pl.semaphore_wait(pltpu.get_barrier_semaphore(), count + 1)
+    height = free.shape[1] // LANES
+    inner = ((x, 2), (cot, 1))
+    copies = []
+    for which, (out, rim) in enumerate(inner):
+        for j in range(1, count):
+            peer = lax.rem(me + j, count)
+            copy = remote(
+                packed.at[peer, which],
+                out.at[me, :, rim * LANES : (rim + height) * LANES],
+                send.at[which, j],
+                recv.at[which, j],
+                orient=peer,
+            )
+            copy.start()
+            copies.append(copy)
+
+    def rims(kind, out, rim, lead):
+        size = rim * LANES
+        end = (rim + height) * LANES
+        up = remote(
+            out.at[lead + (slice(size, 2 * size),)],
+            out.at[lead + (slice(end, end + size),)],
+            edge_send.at[0, kind],
+            edge_recv.at[0, kind],
+            strip=lax.rem(z + strips - 1, strips),
+        )
+        down = remote(
+            out.at[lead + (slice(end - size, end),)],
+            out.at[lead + (slice(0, size),)],
+            edge_send.at[1, kind],
+            edge_recv.at[1, kind],
+            strip=lax.rem(z + 1, strips),
+        )
+
+        @pl.when(z > 0)
+        def _():
+            up.start()
+
+        @pl.when(z == 0)
+        def _():
+            out[lead + (slice(0, size),)] = jnp.zeros(out.shape[:-1] + (size,), out.dtype)
+
+        @pl.when(z < strips - 1)
+        def _():
+            down.start()
+
+        @pl.when(z == strips - 1)
+        def _():
+            out[lead + (slice(end, end + size),)] = jnp.zeros(out.shape[:-1] + (size,), out.dtype)
+
+        return up, down
+
+    opened[:, LANES : (1 + height) * LANES] = free[...]
+    pairs = [rims(2, opened, 1, (slice(None),))]
+    for which, (out, rim) in enumerate(inner):
+        out[me, :, rim * LANES : (rim + height) * LANES] = packed[me, which]
+    for which, (out, rim) in enumerate(inner):
+        for copy in copies[which * (count - 1) : (which + 1) * (count - 1)]:
+            copy.wait_recv()
+        pairs.append(rims(which, out, rim, (slice(None), slice(None))))
+    for copy in copies:
+        copy.wait_send()
+    for up, down in pairs:
+
+        @pl.when(z > 0)
+        def _():
+            up.wait_send()
+            down.wait_recv()
+
+        @pl.when(z < strips - 1)
+        def _():
+            down.wait_send()
+            up.wait_recv()
+
+
+def exchange_in_kernel(packed, free):
+    vmem = pl.BlockSpec(memory_space=pltpu.VMEM)
+    count, _, local, lanes = packed.shape
+    return pl.pallas_call(
+        functools.partial(exchange_in, count, lax.axis_size("strip")),
+        out_shape=(
+            jax.ShapeDtypeStruct((count, local, lanes + 4 * LANES), BF16),
+            jax.ShapeDtypeStruct((count, local, lanes + 2 * LANES), BF16),
+            jax.ShapeDtypeStruct((8, lanes + 2 * LANES), F32),
+        ),
+        in_specs=[vmem] * 2,
+        out_specs=(vmem,) * 3,
+        scratch_shapes=[
+            pltpu.SemaphoreType.DMA((2, count)),
+            pltpu.SemaphoreType.DMA((2, count)),
+            pltpu.SemaphoreType.DMA((2, 3)),
+            pltpu.SemaphoreType.DMA((2, 3)),
+        ],
+        compiler_params=pltpu.CompilerParams(
+            collective_id=0, has_side_effects=True, vmem_limit_bytes=32 * 1024 * 1024
+        ),
+    )(packed, free)
+
+
+def exchange_out(count, strips, wake, shares, out, full, parts, totals, done, send, recv, z_send, z_recv):
+    me, z = lax.axis_index("orient"), lax.axis_index("strip")
+    for j in range(1, count):
+        greet(orient=lax.rem(me + j, count))
+    for j in range(1, strips):
+        greet(strip=lax.rem(z + j, strips))
+    pl.semaphore_wait(pltpu.get_barrier_semaphore(), count + strips - 2)
+
+    def to_all(kind, src_of, dst):
+        copies = []
+        for j in range(1, count):
+            peer = lax.rem(me + j, count)
+            copy = remote(
+                src_of(peer), dst.at[me], send.at[kind, j], recv.at[kind, j], orient=peer
+            )
+            copy.start()
+            copies.append(copy)
+        return copies
+
+    first = to_all(0, lambda peer: shares.at[peer], parts)
+    waking = to_all(1, lambda peer: wake.at[peer], out)
+    parts[me] = shares[me]
+    out[me] = wake[me]
+    for copy in first:
+        copy.wait_recv()
+    total = parts[0]
+    for i in range(1, count):
+        total = total + parts[i]
+    totals[z] = total
+    second = []
+    for j in range(1, strips):
+        copy = remote(
+            totals.at[z], totals.at[z], z_send.at[j], z_recv.at[j], strip=lax.rem(z + j, strips)
+        )
+        copy.start()
+        second.append(copy)
+    for copy in second:
+        copy.wait_recv()
+    total = totals[0]
+    for i in range(1, strips):
+        total = total + totals[i]
+    done[...] = total
+    full[me] = total
+    third = to_all(2, lambda peer: done, full)
+    for copy in third + waking:
+        copy.wait_recv()
+    for copy in first + waking + second + third:
+        copy.wait_send()
+
+
+def exchange_out_kernel(wake, shares):
+    vmem = pl.BlockSpec(memory_space=pltpu.VMEM)
+    count, strips = wake.shape[0], lax.axis_size("strip")
+    part = shares.shape[1:]
+    return pl.pallas_call(
+        functools.partial(exchange_out, count, strips),
+        out_shape=(
+            jax.ShapeDtypeStruct(wake.shape, wake.dtype),
+            jax.ShapeDtypeStruct(shares.shape, F32),
+        ),
+        in_specs=[vmem] * 2,
+        out_specs=(vmem,) * 2,
+        scratch_shapes=[
+            pltpu.VMEM((count,) + part, F32),
+            pltpu.VMEM((strips,) + part, F32),
+            pltpu.VMEM(part, F32),
+            pltpu.SemaphoreType.DMA((3, count)),
+            pltpu.SemaphoreType.DMA((3, count)),
+            pltpu.SemaphoreType.DMA((strips,)),
+            pltpu.SemaphoreType.DMA((strips,)),
+        ],
+        compiler_params=pltpu.CompilerParams(
+            collective_id=1, has_side_effects=True, vmem_limit_bytes=32 * 1024 * 1024
+        ),
+    )(wake, shares)
 
 
 def shards(inflow_field, kernel_one, kernel_two, turbine_mask, wind_sector, wake_cotangent):
@@ -279,18 +460,18 @@
     free = jnp.pad((1 - turbine_mask).astype(F32), ((0, 0), (2, LANES)))
     free = lax.dynamic_slice_in_dim(free, lax.axis_index("orient") * width, LANES, axis=1)
     free = jnp.where(jnp.arange(LANES) < width + 4, free, 0.0)
-    free = edges(free, 1)
-    opened = jnp.broadcast_to(free.reshape(1, -1), (8, (height + 2) * LANES))
-    spread = lax.all_to_all(packed, "orient", 0, 0, tiled=True)
-    spread = spread.reshape(devices, 2, local, height, LANES)
-    x = edges(spread[:, 0], 2).reshape(devices * local, -1)
-    cot = edges(spread[:, 1], 1).reshape(devices * local, -1)
+    free = jnp.broadcast_to(free.reshape(1, -1), (8, height * LANES))
+    x, cot, opened = exchange_in_kernel(packed, free)
+    x = x.reshape(devices * local, -1)
+    cot = cot.reshape(devices * local, -1)
     bank1, bank2 = kernel_one.reshape(-1, channels), kernel_two.reshape(-1, channels)
     wake, shares = local_kernel(width, wind_sector, bank1, bank2, opened, x, cot)
-    wake = lax.all_to_all(wake.reshape(devices, local, -1), "orient", 0, 0, tiled=True)
+    wake, shares = exchange_out_kernel(
+        wake.reshape(devices, local, -1), shares.reshape(devices, -1, LANES)
+    )
     wake = wake.reshape(devices, local, height, LANES)[..., 2 : 2 + extent // devices]
     wake = wake.transpose(1, 2, 0, 3).reshape(groups, channels, height, extent)
-    one, two = expand_kernel(scale, summed(shares))
+    one, two = expand_kernel(scale, shares.reshape(144, 256))
     return (wake, one.reshape(kernel_one.shape), two.reshape(kernel_two.shape))
 
 

time: 93.3 us -> 56 us (0.60)
  Pallas kernels: 12.4 us -> 46.7 us
  waiting for transfers between devices: 29.6 us -> 0 us
  starting transfers between devices: 27.2 us -> 0 us
  blocking collectives: 11.4 us -> 0 us
  local copies, waits for them, and re-layouts: 8.93 us -> 6.89 us
  other arithmetic: 1.81 us -> 0.81 us
    pallas_call x0 -> x2, Pallas kernels: none -> 35.9 us  [the longest x1 20.9 us: exchange_in_kernel(): pl.pallas_call(functools.partial(exchange_in, count, lax.axis_size('strip...]
    all_to_all x3 -> x0, waiting for transfers between devices: 22.4 us -> none  [the longest x1 9.57 us: shards(): lax.all_to_all(wake.reshape(devices, local, -1), 'orient', 0, 0, tiled=True)]
    ppermute x6 -> x0, starting transfers between devices: 15.6 us -> none  [the longest x3 11.5 us: edges(): before = lax.ppermute(rows[..., height - width:, :], 'strip', up)]
    all_to_all x3 -> x0, starting transfers between devices: 11.6 us -> none  [the longest x1 5.3 us: shards(): spread = lax.all_to_all(packed, 'orient', 0, 0, tiled=True)]
    all_to_all x1 -> x0, blocking collectives: 11.4 us -> none  [summed(): parts = lax.all_to_all(shares.reshape(count, -1), axes, 0, 0, tiled=True)]
    ppermute x6 -> x0, waiting for transfers between devices: 7.17 us -> none  [the longest x3 7.02 us: edges(): after = lax.ppermute(rows[..., :width, :], 'strip', down)]
    concatenate x2 -> x0, other arithmetic: 1.26 us -> none  [edges(): return jnp.concatenate([before, rows, after], axis=-2)]
    unnamed x19 -> x13, local copies, waits for them, and re-layouts: 6.22 us -> 4.97 us
  transfers between devices with their start and end apart: 9 -> 0, of which waited for: 6 -> 0; matrix products, arithmetic and copies ran while one was open for 4% -> 0% of each run, Pallas kernels for 0% -> 0%
where the time goes in v3:
time: 56 us; the launch traced here: 55.8 us
  Pallas kernels  46.7 us (83%)
  local copies, waits for them, and re-layouts  6.89 us (12%)
  between operations  1.4 us (2%)
  other arithmetic  0.81 us (1%)
    pallas_call x1, Pallas kernels, exchange_in_kernel(): pl.pallas_call(functools.partial(exchange_in, count, lax.axis_size('strip...  20.9 us
    pallas_call x1, Pallas kernels, exchange_out_kernel(): pl.pallas_call(functools.partial(exchange_out, count, strips), out_shape=...  15 us
    pallas_call x1, Pallas kernels, local_kernel(): pl.pallas_call(functools.partial(compute, width), out_shape=(jax.ShapeDty...  9.65 us
    unnamed x13, local copies, waits for them, and re-layouts  4.97 us

profile of v3, /device:TPU:0, one launch (start us, length us, event | category | flops | bytes accessed | tf_op | source)
XLA Modules:
  0.0 55.8 jit_solution(11414490463596466679)
XLA Ops:
  0.6 0.7 %subtract_convert_fusion = f32[8,512]{1,0:T(8,128)S(1)} fusion(s32[8,512]{1,0:T(8,128)} %param.9), kind=kLoop, calls=%fused_computation.2 | loop fusion | flops 8192 | bytes 32768 | tf_op jit(solution)/shard_map/convert_element_type | solution.py:460
  1.4 0.1 fusion.1
  1.5 0.0 copy-start
  1.5 0.9 %copy-done = bf16[4,8,8,512]{3,2,1,0:T(8,128)(2,1)S(1)} copy-done((bf16[4,8,8,512]{3,2,1,0:T(8,128)(2,1)S(1)}, bf16[4,8,8,512]{3,2,1,0:T(8,128)(2,1)}, u32[]{:S(2)}) %copy-start) | copy-done | bytes 262168
  2.4 0.0 copy-start.1
  2.4 0.9 %copy-done.1 = bf16[4,8,8,512]{3,2,1,0:T(8,128)(2,1)S(1)} copy-done((bf16[4,8,8,512]{3,2,1,0:T(8,128)(2,1)S(1)}, bf16[4,8,8,512]{3,2,1,0:T(8,128)(2,1)}, u32[]{:S(2)}) %copy-start.1) | copy-done | bytes 262168
  3.4 0.0 copy-start.2
  3.4 0.5 shard_map.85.packed
  3.9 0.0 copy-start.3
  3.9 20.9 %shard_map.86 = (bf16[8,32,1536]{2,1,0:T(8,128)(2,1)S(1)}, bf16[8,32,1280]{2,1,0:T(8,128)(2,1)S(1)}, f32[8,1280]{1,0:T(8,128)S(1)}) custom-call(bf16[8,2,32,1024]{3,2,1,0:T(8,128)(2,1)S(1)} %shard_map.85.packed, f32[8,1024]{1,0:T(8,128)S(1)} %broadcast_in_dim.18.free), custom_call_target="tpu_custom_call" | custom-call | tf_op jit(solution)/shard_map/pallas_call | solution.py:354
  24.8 0.0 copy-done.2
  24.8 0.4 copy.14
  25.2 0.0 copy-done.3
  25.2 0.4 copy.15
  26.3 9.6 %shard_map.87 = (bf16[256,1024]{1,0:T(8,128)(2,1)S(1)}, f32[144,256]{1,0:T(8,128)S(1)}) custom-call(s32[1]{0:T(128)S(6)} %copy.20.sector, bf16[2304,8]{1,0:T(8,128)(2,1)S(1)} %bitcast.19, bf16[2304,8]{1,0:T(8,128)(2,1)S(1)} %bitcast.20, f32[8,1280]{1,0:T(8,128)S(1)} %get-tuple-element.12.opened, bf16[256,1536]{1,0:T(8,128)(2,1)S(1)} %bitcast.23, ...), custom_call_target="tpu_custom_call" | custom-call | tf_op jit(solution)/shard_map/pallas_call | solution.py:225
  36.0 15.0 %shard_map.88 = (bf16[8,32,1024]{2,1,0:T(8,128)(2,1)S(1)}, f32[8,36,128]{2,1,0:T(8,128)S(1)}) custom-call(bf16[8,32,1024]{2,1,0:T(8,128)(2,1)S(1)} %bitcast.26, f32[8,36,128]{2,1,0:T(8,128)S(1)} %reshape.54.shares), custom_call_target="tpu_custom_call" | custom-call | tf_op jit(solution)/shard_map/pallas_call | solution.py:429
  51.0 0.6 %shard_map.89 = (f32[2304,8]{1,0:T(8,128)S(1)}, f32[2304,8]{1,0:T(8,128)S(1)}) custom-call(f32[144,256]{1,0:T(8,128)S(1)} %reshape.57.shares), custom_call_target="tpu_custom_call" | custom-call | tf_op jit(solution)/shard_map/pallas_call | solution.py:186
  51.6 1.1 %copy.17 = f32[32,9,8,8]{0,3,2,1:T(8,128)} copy(f32[32,9,8,8]{3,2,1,0:T(8,128)S(1)} %bitcast.22) | data formatting | bytes 147456
  52.7 1.1 %copy.18 = f32[32,9,8,8]{0,3,2,1:T(8,128)} copy(f32[32,9,8,8]{3,2,1,0:T(8,128)S(1)} %bitcast.21) | data formatting | bytes 147456
  53.8 0.1 copy.19
  53.9 0.2 slice_bitcast_fusion
  54.1 0.6 %copy.16 = bf16[32,8,8,64]{3,2,1,0:T(8,128)(2,1)S(1)} copy(bf16[32,8,8,64]{3,1,0,2:T(8,128)(2,1)S(1)} %slice_bitcast_fusion) | data formatting | bytes 524288 | tf_op jit(solution)/shard_map/transpose | solution.py:473
  54.7 1.0 %reshape.56 = bf16[4,8,8,512]{3,2,1,0:T(8,128)(2,1)} reshape(bf16[32,8,8,64]{3,2,1,0:T(8,128)(2,1)S(1)} %copy.16) | data formatting | bytes 524288 | tf_op jit(solution)/shard_map/reshape | solution.py:473
  (4 shorter events, 0.1 us)
Async XLA Ops:
  1.5 0.9 %copy-start = (bf16[4,8,8,512]{3,2,1,0:T(8,128)(2,1)S(1)}, bf16[4,8,8,512]{3,2,1,0:T(8,128)(2,1)}, u32[]{:S(2)}) copy-start(bf16[4,8,8,512]{3,2,1,0:T(8,128)(2,1)} %param.6) | copy-start | bytes 786436
  2.4 0.9 %copy-start.1 = (bf16[4,8,8,512]{3,2,1,0:T(8,128)(2,1)S(1)}, bf16[4,8,8,512]{3,2,1,0:T(8,128)(2,1)}, u32[]{:S(2)}) copy-start(bf16[4,8,8,512]{3,2,1,0:T(8,128)(2,1)} %param.11) | copy-start | bytes 786436
  3.4 21.5 %copy-start.2 = (bf16[32,9,8,8]{0,3,2,1:T(8,128)(2,1)S(1)}, bf16[32,9,8,8]{0,3,2,1:T(8,128)(2,1)}, u32[]{:S(2)}) copy-start(bf16[32,9,8,8]{0,3,2,1:T(8,128)(2,1)} %param.7) | copy-start | bytes 110596
  3.9 21.3 %copy-start.3 = (bf16[32,9,8,8]{0,3,2,1:T(8,128)(2,1)S(1)}, bf16[32,9,8,8]{0,3,2,1:T(8,128)(2,1)}, u32[]{:S(2)}) copy-start(bf16[32,9,8,8]{0,3,2,1:T(8,128)(2,1)} %param.8) | copy-start | bytes 110596

commit v4 on v3

--- a/solution.py
+++ b/solution.py
@@ -177,12 +177,12 @@
     for layer, out in enumerate((one, two)):
         value = shares[layer * 72 : (layer + 1) * 72, :] * scale
         for e in range(G):
-            out[e * 72 : (e + 1) * 72, :] = value[:, e * 8 : e * 8 + 8]
+            out[e] = value[:, e * 8 : e * 8 + 8].reshape(9, 8, 8)
 
 
 def expand_kernel(scale, shares):
     vmem = pl.BlockSpec(memory_space=pltpu.VMEM)
-    out = jax.ShapeDtypeStruct((G * 72, 8), F32)
+    out = jax.ShapeDtypeStruct((G, 9, 8, 8), F32)
     return pl.pallas_call(
         functools.partial(expand, scale),
         out_shape=(out, out),
@@ -472,7 +472,7 @@
     wake = wake.reshape(devices, local, height, LANES)[..., 2 : 2 + extent // devices]
     wake = wake.transpose(1, 2, 0, 3).reshape(groups, channels, height, extent)
     one, two = expand_kernel(scale, shares.reshape(144, 256))
-    return (wake, one.reshape(kernel_one.shape), two.reshape(kernel_two.shape))
+    return (wake, one, two)
 
 
 def solution(mesh):

time: 56 us -> 56 us (level)
  no operation moved by 1% of the time
where the time goes in v4:
time: 56 us; the launch traced here: 55.8 us
  Pallas kernels  46.7 us (83%)
  local copies, waits for them, and re-layouts  6.89 us (12%)
  between operations  1.4 us (2%)
  other arithmetic  0.81 us (1%)
    pallas_call x1, Pallas kernels, exchange_in_kernel(): pl.pallas_call(functools.partial(exchange_in, count, lax.axis_size('strip...  20.9 us
    pallas_call x1, Pallas kernels, exchange_out_kernel(): pl.pallas_call(functools.partial(exchange_out, count, strips), out_shape=...  15 us
    pallas_call x1, Pallas kernels, local_kernel(): pl.pallas_call(functools.partial(compute, width), out_shape=(jax.ShapeDty...  9.65 us
    unnamed x13, local copies, waits for them, and re-layouts  4.97 us

profile of v4, /device:TPU:0, one launch (start us, length us, event | category | flops | bytes accessed | tf_op | source)
XLA Modules:
  0.0 55.8 jit_solution(11414490463596466679)
XLA Ops:
  0.6 0.7 %subtract_convert_fusion = f32[8,512]{1,0:T(8,128)S(1)} fusion(s32[8,512]{1,0:T(8,128)} %param.9), kind=kLoop, calls=%fused_computation.2 | loop fusion | flops 8192 | bytes 32768 | tf_op jit(solution)/shard_map/convert_element_type | solution.py:460
  1.4 0.1 fusion.1
  1.5 0.0 copy-start
  1.5 0.9 %copy-done = bf16[4,8,8,512]{3,2,1,0:T(8,128)(2,1)S(1)} copy-done((bf16[4,8,8,512]{3,2,1,0:T(8,128)(2,1)S(1)}, bf16[4,8,8,512]{3,2,1,0:T(8,128)(2,1)}, u32[]{:S(2)}) %copy-start) | copy-done | bytes 262168
  2.4 0.0 copy-start.1
  2.4 0.9 %copy-done.1 = bf16[4,8,8,512]{3,2,1,0:T(8,128)(2,1)S(1)} copy-done((bf16[4,8,8,512]{3,2,1,0:T(8,128)(2,1)S(1)}, bf16[4,8,8,512]{3,2,1,0:T(8,128)(2,1)}, u32[]{:S(2)}) %copy-start.1) | copy-done | bytes 262168
  3.4 0.0 copy-start.2
  3.4 0.5 shard_map.85.packed
  3.9 0.0 copy-start.3
  3.9 20.9 %shard_map.86 = (bf16[8,32,1536]{2,1,0:T(8,128)(2,1)S(1)}, bf16[8,32,1280]{2,1,0:T(8,128)(2,1)S(1)}, f32[8,1280]{1,0:T(8,128)S(1)}) custom-call(bf16[8,2,32,1024]{3,2,1,0:T(8,128)(2,1)S(1)} %shard_map.85.packed, f32[8,1024]{1,0:T(8,128)S(1)} %broadcast_in_dim.18.free), custom_call_target="tpu_custom_call" | custom-call | tf_op jit(solution)/shard_map/pallas_call | solution.py:354
  24.8 0.0 copy-done.2
  24.8 0.4 copy.14
  25.2 0.0 copy-done.3
  25.2 0.4 copy.15
  26.3 9.6 %shard_map.87 = (bf16[256,1024]{1,0:T(8,128)(2,1)S(1)}, f32[144,256]{1,0:T(8,128)S(1)}) custom-call(s32[1]{0:T(128)S(6)} %copy.20.sector, bf16[2304,8]{1,0:T(8,128)(2,1)S(1)} %bitcast.17, bf16[2304,8]{1,0:T(8,128)(2,1)S(1)} %bitcast.18, f32[8,1280]{1,0:T(8,128)S(1)} %get-tuple-element.12.opened, bf16[256,1536]{1,0:T(8,128)(2,1)S(1)} %bitcast.19, ...), custom_call_target="tpu_custom_call" | custom-call | tf_op jit(solution)/shard_map/pallas_call | solution.py:225
  36.0 15.0 %shard_map.88 = (bf16[8,32,1024]{2,1,0:T(8,128)(2,1)S(1)}, f32[8,36,128]{2,1,0:T(8,128)S(1)}) custom-call(bf16[8,32,1024]{2,1,0:T(8,128)(2,1)S(1)} %bitcast.22, f32[8,36,128]{2,1,0:T(8,128)S(1)} %reshape.48.shares), custom_call_target="tpu_custom_call" | custom-call | tf_op jit(solution)/shard_map/pallas_call | solution.py:429
  51.0 0.6 %shard_map.89 = (f32[32,9,8,8]{3,2,1,0:T(8,128)S(1)}, f32[32,9,8,8]{3,2,1,0:T(8,128)S(1)}) custom-call(f32[144,256]{1,0:T(8,128)S(1)} %reshape.51.shares), custom_call_target="tpu_custom_call" | custom-call | tf_op jit(solution)/shard_map/pallas_call | solution.py:186
  51.6 1.1 %copy.17 = f32[32,9,8,8]{0,3,2,1:T(8,128)} copy(f32[32,9,8,8]{3,2,1,0:T(8,128)S(1)} %get-tuple-element.25) | data formatting | bytes 147456
  52.7 1.1 %copy.18 = f32[32,9,8,8]{0,3,2,1:T(8,128)} copy(f32[32,9,8,8]{3,2,1,0:T(8,128)S(1)} %get-tuple-element.26) | data formatting | bytes 147456
  53.8 0.1 copy.19
  53.9 0.2 slice_bitcast_fusion
  54.1 0.6 %copy.16 = bf16[32,8,8,64]{3,2,1,0:T(8,128)(2,1)S(1)} copy(bf16[32,8,8,64]{3,1,0,2:T(8,128)(2,1)S(1)} %slice_bitcast_fusion) | data formatting | bytes 524288 | tf_op jit(solution)/shard_map/transpose | solution.py:473
  54.7 1.0 %reshape.50 = bf16[4,8,8,512]{3,2,1,0:T(8,128)(2,1)} reshape(bf16[32,8,8,64]{3,2,1,0:T(8,128)(2,1)S(1)} %copy.16) | data formatting | bytes 524288 | tf_op jit(solution)/shard_map/reshape | solution.py:473
  (4 shorter events, 0.1 us)
Async XLA Ops:
  1.5 0.9 %copy-start = (bf16[4,8,8,512]{3,2,1,0:T(8,128)(2,1)S(1)}, bf16[4,8,8,512]{3,2,1,0:T(8,128)(2,1)}, u32[]{:S(2)}) copy-start(bf16[4,8,8,512]{3,2,1,0:T(8,128)(2,1)} %param.6) | copy-start | bytes 786436
  2.4 0.9 %copy-start.1 = (bf16[4,8,8,512]{3,2,1,0:T(8,128)(2,1)S(1)}, bf16[4,8,8,512]{3,2,1,0:T(8,128)(2,1)}, u32[]{:S(2)}) copy-start(bf16[4,8,8,512]{3,2,1,0:T(8,128)(2,1)} %param.11) | copy-start | bytes 786436
  3.4 21.5 %copy-start.2 = (bf16[32,9,8,8]{0,3,2,1:T(8,128)(2,1)S(1)}, bf16[32,9,8,8]{0,3,2,1:T(8,128)(2,1)}, u32[]{:S(2)}) copy-start(bf16[32,9,8,8]{0,3,2,1:T(8,128)(2,1)} %param.7) | copy-start | bytes 110596
  3.9 21.3 %copy-start.3 = (bf16[32,9,8,8]{0,3,2,1:T(8,128)(2,1)S(1)}, bf16[32,9,8,8]{0,3,2,1:T(8,128)(2,1)}, u32[]{:S(2)}) copy-start(bf16[32,9,8,8]{0,3,2,1:T(8,128)(2,1)} %param.8) | copy-start | bytes 110596
